TPU v7x, 32 devices: a whole 2x2x4 slice. The times are simulated.
32 devices in a mesh: section: 2 (over core), dp: 4 (over z), seq: 4 (over y, x).
Axes of the slice: x: 2, y: 2, z: 4, core: 2. Of those that a mesh axis runs over, the one named last changes fastest.
Arguments:
- enc_states: bfloat16 [8, 512, 4096], P(('section', 'dp'), 'seq'), may hold values from -6 to 6
- enc_gain: float32 [4096], replicated, may hold values from 0.1 to 1.9
- key_weight: bfloat16 [4096, 4096], P(None, 'seq'), may hold values from -0.09375 to 0.09375
- value_weight: bfloat16 [4096, 4096], P(None, 'seq'), may hold values from -0.09375 to 0.09375
- queries: bfloat16 [8, 512, 4096], P(('section', 'dp'), None, 'seq'), may hold values from -28 to 28
- out_grad: bfloat16 [8, 512, 4096], P(('section', 'dp'), None, 'seq'), may hold values from -6 to 6
- lengths: int32 [8], replicated, may hold values from 256 to 512, as said below
Outputs:
- attended: bfloat16 [8, 512, 4096], P(('section', 'dp'), None, 'seq')
- enc_grad: bfloat16 [8, 512, 4096], P(('section', 'dp'), 'seq')
- key_grad: float32 [4096, 4096], P(('section', 'dp'), 'seq')
- value_grad: float32 [4096, 4096], P(('section', 'dp'), 'seq')
- query_grad: bfloat16 [8, 512, 4096], P(('section', 'dp'), None, 'seq')
Inputs may be any that keep to these rules, and one draw needn't show every extreme that they name: `lengths`: positions at or beyond a sequence's length are padding; at least one sequence in every draw has length 512.
All inputs are finite; a program needn't handle non-finite values.
Results may differ from a plain program's by a relative error of at most 0.023.
The roundings to bfloat16 on the way count: a program that leaves them out, or rounds other values in their place, can miss the bound.
Values may be sent and summed in bfloat16 or wider, within the bound.
No kernel may reach another device: no remote copies, remote signals or barrier semaphores. Data moves between devices by JAX's collectives and lax.ppermute only.
A program may use at most 128 MiB of HBM per device.

v0:
```python
import functools

import jax
import jax.numpy as jnp
from jax import lax
from jax.experimental import pallas as pl
from jax.experimental.pallas import tpu as pltpu
from jax.sharding import PartitionSpec as P

HD = 256


EPS = 1e-06
NEG_FILL = -1e30
BF16 = jnp.bfloat16
F32 = jnp.float32
MIB = 1024 * 1024
FILLS_WAITS = pl.CostEstimate(flops=0, bytes_accessed=0, transcendentals=0)


def swap(value, axis, mask):
    pairs = [(source, source ^ mask) for source in range(lax.axis_size(axis))]
    return lax.ppermute(value, axis, pairs)


def normalize(enc_rows, gain):
    wide_rows = enc_rows.astype(F32)
    factor = lax.rsqrt(jnp.mean(wide_rows * wide_rows, axis=-1, keepdims=True) + EPS)
    return ((wide_rows * factor * gain).astype(BF16), factor)


def norm_backward(enc_rows, factor, gain, row_grad):
    wide_rows = enc_rows.astype(F32)
    scaled = row_grad.astype(F32) * gain
    inner_sum = jnp.mean(scaled * wide_rows, axis=-1, keepdims=True)
    return (factor * scaled - wide_rows * factor * factor * factor * inner_sum).astype(BF16)


def tie(*values):
    return lax.optimization_barrier(values)


def dot(left, right, left_dim, right_dim):
    return lax.dot_general(
        left, right, (((left_dim,), (right_dim,)), ((), ())), preferred_element_type=F32
    )


def attend_kernel(
    visible, query, key_early, key_late, value_early, value_late, upstream, attended, query_grad, kv_grad
):
    score_scale = HD ** (-0.5)
    query_rows, upstream_rows = query[...], upstream[...]
    key_rows = jnp.concatenate([key_early[...], key_late[...]], axis=0)
    value_rows = jnp.concatenate([value_early[...], value_late[...]], axis=0)
    scores = dot(key_rows, query_rows, 1, 1) * score_scale
    scores = jnp.where(visible[...] > 0, scores, NEG_FILL)
    exponent = jnp.exp(scores - jnp.max(scores, axis=0, keepdims=True))
    probability = exponent * (1.0 / jnp.sum(exponent, axis=0, keepdims=True))
    prob_weights = probability.astype(BF16)
    grad_probs = dot(value_rows, upstream_rows, 1, 1)
    inner_sum = jnp.sum(probability * grad_probs, axis=0, keepdims=True)
    grad_scores = (probability * (grad_probs - inner_sum) * score_scale).astype(BF16)
    kv_grad[:, :HD] = dot(grad_scores, query_rows, 1, 0).astype(BF16)
    kv_grad[:, HD:] = dot(prob_weights, upstream_rows, 1, 0).astype(BF16)
    attended[...] = dot(prob_weights, value_rows, 0, 0).astype(BF16)
    query_grad[...] = dot(grad_scores, key_rows, 0, 0).astype(BF16)


def attend_head(head, visible, query, key_early, key_late, value_early, value_late, upstream):
    src_rows, target_rows = visible.shape[0], query.shape[0]
    early, late = key_early.shape[0], key_late.shape[0]

    def column(rows):
        return pl.BlockSpec((rows, HD), lambda step: (0, head))

    def whole(rows, columns):
        return pl.BlockSpec((rows, columns), lambda step: (0, 0))

    return pl.pallas_call(
        attend_kernel,
        grid=(1,),
        in_specs=[
            whole(src_rows, 1),
            column(target_rows),
            column(early),
            column(late),
            column(early),
            column(late),
            column(target_rows),
        ],
        out_specs=[whole(target_rows, HD), whole(target_rows, HD), whole(src_rows, 2 * HD)],
        out_shape=[
            jax.ShapeDtypeStruct((target_rows, HD), BF16),
            jax.ShapeDtypeStruct((target_rows, HD), BF16),
            jax.ShapeDtypeStruct((src_rows, 2 * HD), BF16),
        ],
        compiler_params=pltpu.CompilerParams(vmem_limit_bytes=6 * MIB + 40 * src_rows * target_rows),
        cost_estimate=FILLS_WAITS,
    )(visible, query, key_early, key_late, value_early, value_late, upstream)


def row_kernel(head_count, *refs):
    grads, (key_block, value_block), out = refs[:head_count], refs[head_count : head_count + 2], refs[-1]
    key_grads = jnp.concatenate([grad[:, :HD] for grad in grads], axis=1)
    value_grads = jnp.concatenate([grad[:, HD:] for grad in grads], axis=1)
    out[...] = (dot(key_grads, key_block[...], 1, 1) + dot(value_grads, value_block[...], 1, 1)).astype(BF16)


def row_product(grads, key_weight, value_weight, part, parts):
    rows, columns = grads[0].shape
    features, heads_width = key_weight.shape
    block = 512
    steps = features // block // parts
    first = part * steps
    whole = pl.BlockSpec((rows, columns), lambda step: (0, 0))
    weight = pl.BlockSpec((block, heads_width), lambda step: (first + step, 0))
    return pl.pallas_call(
        functools.partial(row_kernel, len(grads)),
        grid=(steps,),
        in_specs=[whole] * len(grads) + [weight, weight],
        out_specs=pl.BlockSpec((rows, block), lambda step: (0, step)),
        out_shape=jax.ShapeDtypeStruct((rows, features // parts), BF16),
        compiler_params=pltpu.CompilerParams(vmem_limit_bytes=14 * MIB + 12 * rows * block),
        cost_estimate=pl.CostEstimate(
            flops=4 * rows * features * heads_width // parts,
            bytes_accessed=(4 * features * heads_width + 2 * rows * (features + 2 * heads_width)) // parts,
            transcendentals=0,
        ),
    )(*grads, key_weight, value_weight)


def add_kernel(kind_count, local, first, second, *refs):
    outs = refs[-kind_count:]
    total = local[...] + first[...].astype(F32) + second[...].astype(F32)
    for slot, out in enumerate(outs):
        out[...] = total[:, slot * HD : (slot + 1) * HD]


def add_columns(totals, head, heads_here, local, first, second):
    rows, columns = local.shape
    here = pl.BlockSpec((rows, columns), lambda step: (0, 0))
    kept = [total for total in totals if total is not None]
    count = columns // HD
    return pl.pallas_call(
        functools.partial(add_kernel, count),
        grid=(1,),
        in_specs=[here] * 3 + [pl.BlockSpec(memory_space=pl.ANY)] * len(kept),
        out_specs=[pl.BlockSpec((rows, HD), lambda step: (0, head))] * count,
        out_shape=[jax.ShapeDtypeStruct((rows, heads_here * HD), F32)] * count,
        input_output_aliases={3 + slot: slot for slot in range(len(kept))},
        cost_estimate=pl.CostEstimate(
            flops=2 * rows * columns, bytes_accessed=12 * rows * columns, transcendentals=0
        ),
        compiler_params=pltpu.CompilerParams(vmem_limit_bytes=12 * MIB),
    )(local, first, second, *kept)


def on_device(enc_states, enc_gain, key_weight, value_weight, queries, out_grad, lengths):
    enc_rows = enc_states[0]
    own_rows, width = enc_rows.shape
    heads_here = key_weight.shape[1] // HD
    heads = range(heads_here)
    last = heads_here - 1
    section_count, dp_count, seq_count = (lax.axis_size(name) for name in ("section", "dp", "seq"))
    section, place, seq = (lax.axis_index(name) for name in ("section", "dp", "seq"))
    partner = (section * dp_count + place + dp_count) % (section_count * dp_count)
    src_rows = own_rows * seq_count
    section_width = width // section_count
    target_width = section_width // dp_count
    across = [(1, 2), (2, 1)]
    held = {}

    def sync(*names):
        names = ["factor"] + [name for name in names if name in held]
        held.update(zip(names, lax.optimization_barrier(tuple(held[name] for name in names))))

    def section_features(rows, index):
        return lax.dynamic_slice_in_dim(rows, index * section_width, section_width, axis=1)

    def target_features(rows, xors, base=0):
        return jnp.concatenate(
            [
                lax.dynamic_slice_in_dim(rows, base + (place ^ xor) * target_width, target_width, axis=1)
                for xor in xors
            ],
            axis=1,
        )

    def swap_both(rows, mask):
        count = section_count * seq_count
        pairs = [(source, source ^ (seq_count + mask)) for source in range(count)]
        return lax.ppermute(rows, ("section", "seq"), pairs)

    normed, held["factor"] = normalize(enc_rows, enc_gain)
    partner_rows = swap(normed, "section", 1)

    low, high = max(seq_count // 4, 1), max(seq_count // 2, 1)
    if low > 1:
        gathered = []
        for rows in (normed, partner_rows):
            blocks = [rows]
            bit = 1
            while bit < low:
                blocks = blocks + [swap(block, "seq", bit) for block in blocks]
                bit *= 2
            gathered.append(jnp.concatenate(blocks))
        normed, partner_rows = gathered
    half = normed.shape[0] // 2
    first, second = swap_both(normed, low), swap_both(normed, high)

    base = section * section_width
    outer_far = jnp.concatenate([target_features(rows, (3, 2), base) for rows in (partner_rows, normed)])
    outer_far = swap(outer_far, "dp", 1)
    first, second, outer_far = tie(first, second, outer_far)

    third_top, third_bottom = swap(first[:half], "seq", high), swap(second[half:], "seq", low)
    early = jnp.concatenate([partner_rows, first, second])
    away_early = swap(section_features(early[2 * half :], 1 - section), "section", 1)
    value_early = jnp.dot(early, value_weight, preferred_element_type=F32).astype(BF16)
    key_early = jnp.dot(early, key_weight, preferred_element_type=F32).astype(BF16)
    key_early, value_early, away_early, third_top, third_bottom, outer_far = tie(
        key_early, value_early, away_early, third_top, third_bottom, outer_far
    )
    held["first"], held["second"] = swap(outer_far, "seq", low), swap(outer_far, "seq", high)
    late = jnp.concatenate([third_top, third_bottom])
    away_late = swap(section_features(late, 1 - section), "section", 1)
    key_late = jnp.dot(late, key_weight, preferred_element_type=F32).astype(BF16)
    value_late = jnp.dot(late, value_weight, preferred_element_type=F32).astype(BF16)

    block_start = (seq ^ jnp.arange(seq_count, dtype=jnp.int32)) * own_rows
    positions = block_start[:, None] + jnp.arange(own_rows, dtype=jnp.int32)[None, :]
    visible = (positions.reshape(src_rows, 1) < lengths[partner]).astype(jnp.int32)

    held["key_early"] = key_early

    def attend(head):
        held[("attended", head)], held[("query", head)], held[("kv", head)] = attend_head(
            head, visible, queries[0], held["key_early"], key_late, value_early, value_late, out_grad[0]
        )

    def hand_in(head):
        if head < heads_here:
            held[("handed", head)] = swap(held[("kv", head)], "dp", 1)

    def exchange(head):
        held[("their", head)] = swap(held[("kv", head)], "section", 1)

    attend(0)
    hand_in(0)
    exchange(0)
    chip_rows = jnp.concatenate(
        [section_features(early, section), section_features(late, section)]
        + [section_features(normed, section), away_early, away_late]
    )
    held["chip_far"] = target_features(chip_rows, (2, 3))
    held["chip_pair"] = target_features(chip_rows, (1,))
    held["chip_own"] = target_features(chip_rows, (0,))
    sync("first", "second", "key_early", "chip_far", "chip_pair", "chip_own")
    quarter_rows = outer_far.shape[0] // 2
    held["top"] = swap(held["first"][:quarter_rows], "seq", high)
    held["bottom"] = swap(held["second"][quarter_rows:], "seq", low)
    for head in heads[1:]:
        attend(head)
        exchange(head)
    hand_in(1)
    early_pieces = [outer_far, held["first"], held["second"]]
    held["mine"] = jnp.concatenate([piece[:quarter_rows] for piece in early_pieces])
    held["yours"] = jnp.concatenate([piece[quarter_rows:] for piece in early_pieces])
    sync(
        ("handed", 0), ("their", 0), "top", "bottom", "mine", "yours",
        *(("kv", head) for head in heads),
    )

    def chip_sum(name, head):
        rows = held[name]
        return dot(rows[:src_rows], held[("kv", head)], 0, 0) + dot(rows[src_rows:], held[("their", head)], 0, 0)

    def outer_sum(head):
        handed, handed_other = held[("handed", head)], held[("other", head)]
        cut = 3 * quarter_rows
        return (
            dot(held["mine"], handed[:cut], 0, 0)
            + dot(held["yours"], handed_other[:cut], 0, 0)
            + dot(held["top"], handed[cut:], 0, 0)
            + dot(held["bottom"], handed_other[cut:], 0, 0)
        )

    by_steps = seq_count == 4 and heads_here == 4

    def row_block(name, step):
        return held[name][step * own_rows : (step + 1) * own_rows]

    def first_step(name, near, far):
        together = jnp.concatenate([row_block(name, near), row_block(name, far)])
        held[(name, "first")] = swap(together, "seq", near)

    def second_step(name, other):
        passed = row_block(name, other).astype(F32) + held[(name, "first")][own_rows:].astype(F32)
        held[(name, "second")] = swap(passed.astype(BF16), "seq", other)

    def row_total(name):
        total = row_block(name, 0).astype(F32)
        if by_steps:
            first, second = held[(name, "first")][:own_rows], held[(name, "second")]
            return total + first.astype(F32) + second.astype(F32)
        for step in range(1, seq_count):
            total = total + swap(row_block(name, step), "seq", step).astype(F32)
        return total

    def relay(head):
        term = chip_sum("chip_pair", head) + held[("outward", head)].astype(F32)
        held[("relay", head)] = swap(term.astype(BF16), "dp", 1)

    def finish(head):
        totals = [held.get(("total", kind)) for kind in (0, 1)]
        held[("total", 0)], held[("total", 1)] = add_columns(
            totals, head, heads_here, chip_sum("chip_own", head), held[("inner", head)], held[("relay", head)]
        )

    held[("near", 0)] = chip_sum("chip_far", 0)
    held[("other", 0)] = swap(held[("handed", 0)], "section", 1)
    def kinds(*names):
        return [(name, other) for name in names for other in heads]

    for head in heads:
        held["far"] = (held[("near", head)] + outer_sum(head)).astype(BF16)
        sync(
            "far",
            "key_early",
            ("outward", head - 1),
            ("inner", head - 2),
            ("near", head),
            *([("relay", 1)] if head == 3 else []),
            "row_low",
            "row_high",
            *([("row_low", "first")] if head == 2 else [("row_high", "first")] if head == 3 else []),
            *kinds("kv", "their"),
            *((("handed", head + 1),) if head > 0 else ()),
        )
        held[("outward", head)] = lax.ppermute(held["far"][:target_width], "dp", across)
        if head == last:
            sync("far", ("inner", head - 1), *kinds("attended", "query"))
        held[("inner", head)] = lax.ppermute(held["far"][target_width:], "dp", across)
        hand_in(head + 2)
        if head > 0:
            relay(head - 1)
        if head < last:
            if head == 0:
                grads = [held[("kv", other)] for other in heads]
                held["row_low"] = row_product(grads, key_weight, value_weight, 0, 2)
                sync(("outward", 0), ("handed", 1), *kinds("their"))
                held[("near", 1)] = chip_sum("chip_far", 1)
            held[("other", head + 1)] = swap(held[("handed", head + 1)], "section", 1)
            if head > 0:
                sync(
                    ("other", head + 1),
                    ("inner", head - 1),
                    ("relay", head - 2),
                    *kinds("kv", "their"),
                )
                held[("near", head + 1)] = chip_sum("chip_far", head + 1)
        if head == 1:
            if by_steps:
                first_step("row_low", 1, 3)
            grads = [held[("kv", other)] for other in heads]
            held["row_high"] = row_product(grads, key_weight, value_weight, 1, 2)
            if by_steps:
                first_step("row_high", 2, 3)
        if head == 2:
            if by_steps:
                second_step("row_low", 2)
        if head == 3:
            if by_steps:
                second_step("row_high", 1)
    if heads_here == 1:
        held["row_low"] = row_product([held[("kv", 0)]], key_weight, value_weight, 0, 2)
        held["row_high"] = row_product([held[("kv", 0)]], key_weight, value_weight, 1, 2)
    for head in heads[:-1]:
        finish(head)
    sync(("outward", last), *(("relay", head) for head in heads[:-1]))
    relay(last)
    finish(last)

    row_share = jnp.concatenate([row_total("row_low"), row_total("row_high")], axis=1)
    row_grad = swap(row_share.astype(BF16), "section", 1)
    enc_grad = norm_backward(enc_rows, held["factor"], enc_gain, row_grad)
    return (
        jnp.concatenate([held[("attended", head)] for head in heads], axis=1)[None],
        enc_grad[None],
        held[("total", 0)],
        held[("total", 1)],
        jnp.concatenate([held[("query", head)] for head in heads], axis=1)[None],
    )


def solution(mesh):
    placed = (
        P(("section", "dp"), "seq", None),
        P(),
        P(None, "seq"),
        P(None, "seq"),
        P(("section", "dp"), None, "seq"),
        P(("section", "dp"), None, "seq"),
        P(),
    )
    return jax.shard_map(
        on_device,
        mesh=mesh,
        in_specs=placed,
        out_specs=(
            P(("section", "dp"), None, "seq"),
            P(("section", "dp"), "seq", None),
            P(("section", "dp"), "seq"),
            P(("section", "dp"), "seq"),
            P(("section", "dp"), None, "seq"),
        ),
        check_vma=False,
    )
```

profile of v0, /device:TPU:0, one launch (start us, length us, event | category | flops | bytes accessed | tf_op | source)
XLA Modules:
  0.0 194.3 jit_solution(15554079670801104708)
XLA Ops:
  0.6 1.5 fusion
  2.2 1.6 fusion.2
  4.3 2.6 %collective-permute-start.1 = (bf16[128,4096]{1,0:T(8,128)(2,1)S(1)}, bf16[128,4096]{1,0:T(8,128)(2,1)S(1)}, u32[]{:S(2)}, u32[]{:S(2)}) collective-permute-start(bf16[128,4096]{1,0:T(8,128)(2,1)S(1)} %fusion.2), channel_id=1, source_target_pairs={{0,17},{1,16},{2,19},{3,18},{16,1},{17,0},{18,3},{19,2},{4,21},{5,... | collective-permute-start | bytes 3145736 | tf_op jit(solution)/shard_map/ppermute | solution.py:193
  10.6 1.6 collective-permute-start.3
  14.3 16.0 %collective-permute-done.1 = bf16[128,4096]{1,0:T(8,128)(2,1)S(1)} collective-permute-done((bf16[128,4096]{1,0:T(8,128)(2,1)S(1)}, bf16[128,4096]{1,0:T(8,128)(2,1)S(1)}, u32[]{:S(2)}, u32[]{:S(2)}) %collective-permute-start.1) | collective-permute-done | bytes 1048608 | tf_op jit(solution)/shard_map/ppermute | solution.py:193
  30.3 1.8 collective-permute-done.2
  32.7 1.6 collective-permute-start.5
  34.7 7.3 %convolution_convert_fusion.1.key_early = bf16[384,1024]{1,0:T(8,128)(2,1)S(1)} fusion(bf16[384,4096]{1,0:T(8,128)(2,1)S(1)} %constant_dynamic-update-slice_fusion, bf16[4096,1024]{1,0:T(8,128)(2,1)} %refs_4_.3), kind=kOutput, calls=%fused_computation.27 | convolution fusion | flops 3221618688 | bytes 12320768 | tf_op jit(solution)/shard_map/dot_general | solution.py:221
  42.1 3.4 %convolution_convert_fusion.value_early = bf16[384,1024]{1,0:T(8,128)(2,1)S(1)} fusion(bf16[384,4096]{1,0:T(8,128)(2,1)S(1)} %constant_dynamic-update-slice_fusion, bf16[4096,1024]{1,0:T(8,128)(2,1)S(1)} %bitcast.70), kind=kOutput, calls=%fused_computation.26 | convolution fusion | flops 3221618688 | bytes 12320768 | tf_op jit(solution)/shard_map/dot_general | solution.py:220
  53.4 1.9 collective-permute-start.10
  56.4 5.0 %collective-permute-done.7 = bf16[256,1024]{1,0:T(8,128)(2,1)S(1)} collective-permute-done((bf16[256,1024]{1,0:T(8,128)(2,1)}, bf16[256,1024]{1,0:T(8,128)(2,1)S(1)}, u32[]{:S(2)}, u32[]{:S(2)}) %collective-permute-start.7) | collective-permute-done | bytes 524320 | tf_op jit(solution)/shard_map/ppermute | solution.py:23
  62.4 1.6 collective-permute-start.13
  68.0 1.7 shard_map.113
  69.8 1.6 collective-permute-start.19
  77.9 4.4 %collective-permute-start.21 = (bf16[512,512]{1,0:T(8,128)(2,1)S(1)}, bf16[512,512]{1,0:T(8,128)(2,1)S(1)}, u32[]{:S(2)}, u32[]{:S(2)}) collective-permute-start(bf16[512,512]{1,0:T(8,128)(2,1)S(1)} %get-tuple-element.263.refs_2_), channel_id=1, source_target_pairs={{0,4},{4,0},{8,12},{12,8},{1,5},{5,1},{9,13},{13,9},{2,6},{6,2},{1... | collective-permute-start | bytes 1572872 | tf_op jit(solution)/shard_map/ppermute | solution.py:23
  83.0 5.3 %shard_map.114 = bf16[512,2048]{1,0:T(8,128)(2,1)S(1)} custom-call(bf16[512,512]{1,0:T(8,128)(2,1)S(1)} %get-tuple-element.280.refs_0_, bf16[512,512]{1,0:T(8,128)(2,1)S(1)} %get-tuple-element.277.refs_1_, bf16[512,512]{1,0:T(8,128)(2,1)S(1)} %get-tuple-element.263.refs_2_, bf16[512,512]{1,0:T(8,128)(2,1)S(1)} %get-tuple-element.272.refs_3_, ...), custom_call_target="tpu_custom_call" | custom-call | flops 4294967296 | bytes 11534336 | tf_op jit(solution)/shard_map/pallas_call | solution.py:118
  93.3 2.2 %collective-permute-done.21 = bf16[512,512]{1,0:T(8,128)(2,1)S(1)} collective-permute-done((bf16[512,512]{1,0:T(8,128)(2,1)S(1)}, bf16[512,512]{1,0:T(8,128)(2,1)S(1)}, u32[]{:S(2)}, u32[]{:S(2)}) %collective-permute-start.21) | collective-permute-done | bytes 524320 | tf_op jit(solution)/shard_map/ppermute | solution.py:23
  96.3 1.5 collective-permute-start.24
  98.6 7.5 %collective-permute-start.26 = (bf16[512,512]{1,0:T(8,128)(2,1)S(1)}, bf16[512,512]{1,0:T(8,128)(2,1)S(1)}, u32[]{:S(2)}, u32[]{:S(2)}) collective-permute-start(bf16[512,512]{1,0:T(8,128)(2,1)S(1)} %get-tuple-element.272.refs_3_), channel_id=1, source_target_pairs={{0,4},{4,0},{8,12},{12,8},{1,5},{5,1},{9,13},{13,9},{2,6},{6,2},{1... | collective-permute-start | bytes 1572872 | tf_op jit(solution)/shard_map/ppermute | solution.py:23
  111.8 5.5 %shard_map.115 = bf16[512,2048]{1,0:T(8,128)(2,1)S(1)} custom-call(bf16[512,512]{1,0:T(8,128)(2,1)S(1)} %get-tuple-element.280.refs_0_, bf16[512,512]{1,0:T(8,128)(2,1)S(1)} %get-tuple-element.277.refs_1_, bf16[512,512]{1,0:T(8,128)(2,1)S(1)} %get-tuple-element.263.refs_2_, bf16[512,512]{1,0:T(8,128)(2,1)S(1)} %get-tuple-element.272.refs_3_, ...), custom_call_target="tpu_custom_call" | custom-call | flops 4294967296 | bytes 11534336 | tf_op jit(solution)/shard_map/pallas_call | solution.py:118
  119.6 1.5 collective-permute-start.32
  121.1 2.5 %collective-permute-done.25 = bf16[256,2048]{1,0:T(8,128)(2,1)S(1)} collective-permute-done((bf16[256,2048]{1,0:T(8,128)(2,1)S(1)}, bf16[256,2048]{1,0:T(8,128)(2,1)S(1)}, u32[]{:S(2)}, u32[]{:S(2)}) %collective-permute-start.25) | collective-permute-done | bytes 1048608 | tf_op jit(solution)/shard_map/ppermute | solution.py:23
  125.6 1.5 fusion.14
  127.7 8.3 %collective-permute-start.31 = (bf16[512,512]{1,0:T(8,128)(2,1)S(1)}, bf16[512,512]{1,0:T(8,128)(2,1)S(1)}, u32[]{:S(2)}, u32[]{:S(2)}) collective-permute-start(bf16[512,512]{1,0:T(8,128)(2,1)S(1)} %fusion.14), channel_id=1, source_target_pairs={{0,4},{4,0},{8,12},{12,8},{1,5},{5,1},{9,13},{13,9},{2,6},{6,2},{1... | collective-permute-start | bytes 1572872 | tf_op jit(solution)/shard_map/ppermute | solution.py:23
  136.7 1.5 collective-permute-start.36
  141.1 4.6 %collective-permute-done.32 = bf16[256,2048]{1,0:T(8,128)(2,1)S(1)} collective-permute-done((bf16[256,2048]{1,0:T(8,128)(2,1)S(1)}, bf16[256,2048]{1,0:T(8,128)(2,1)S(1)}, u32[]{:S(2)}, u32[]{:S(2)}) %collective-permute-start.32) | collective-permute-done | bytes 1048608 | tf_op jit(solution)/shard_map/ppermute | solution.py:23
  145.8 2.6 %collective-permute-done.31.second = bf16[512,512]{1,0:T(8,128)(2,1)S(1)} collective-permute-done((bf16[512,512]{1,0:T(8,128)(2,1)S(1)}, bf16[512,512]{1,0:T(8,128)(2,1)S(1)}, u32[]{:S(2)}, u32[]{:S(2)}) %collective-permute-start.31) | collective-permute-done | bytes 524320 | tf_op jit(solution)/shard_map/ppermute | solution.py:23
  150.8 11.8 %collective-permute-start.35 = (bf16[512,512]{1,0:T(8,128)(2,1)S(1)}, bf16[512,512]{1,0:T(8,128)(2,1)S(1)}, u32[]{:S(2)}, u32[]{:S(2)}) collective-permute-start(bf16[512,512]{1,0:T(8,128)(2,1)S(1)} %fusion.15), channel_id=1, source_target_pairs={{0,4},{4,0},{8,12},{12,8},{1,5},{5,1},{9,13},{13,9},{2,6},{6,2},{1... | collective-permute-start | bytes 1572872 | tf_op jit(solution)/shard_map/ppermute | solution.py:23
  171.9 1.9 collective-permute-done.35.second
  174.3 3.4 %collective-permute-start.40 = (bf16[512,512]{1,0:T(8,128)(2,1)S(1)}, bf16[512,512]{1,0:T(8,128)(2,1)S(1)}, u32[]{:S(2)}, u32[]{:S(2)}) collective-permute-start(bf16[512,512]{1,0:T(8,128)(2,1)S(1)} %fusion.16), channel_id=1, source_target_pairs={{0,4},{4,0},{8,12},{12,8},{1,5},{5,1},{9,13},{13,9},{2,6},{6,2},{1... | collective-permute-start | bytes 1572872 | tf_op jit(solution)/shard_map/ppermute | solution.py:23
  179.7 10.6 %collective-permute-done.40.second = bf16[512,512]{1,0:T(8,128)(2,1)S(1)} collective-permute-done((bf16[512,512]{1,0:T(8,128)(2,1)S(1)}, bf16[512,512]{1,0:T(8,128)(2,1)S(1)}, u32[]{:S(2)}, u32[]{:S(2)}) %collective-permute-start.40) | collective-permute-done | bytes 524320 | tf_op jit(solution)/shard_map/ppermute | solution.py:23
  192.4 1.7 fusion.18
  (175 shorter events, 65.3 us)
Async XLA Ops:
  4.3 26.1 %collective-permute-start.1 = (bf16[128,4096]{1,0:T(8,128)(2,1)S(1)}, bf16[128,4096]{1,0:T(8,128)(2,1)S(1)}, u32[]{:S(2)}, u32[]{:S(2)}) collective-permute-start(bf16[128,4096]{1,0:T(8,128)(2,1)S(1)} %fusion.2), channel_id=1, source_target_pairs={{0,17},{1,16},{2,19},{3,18},{16,1},{17,0},{18,3},{19,2},{4,21},{5,... | collective-permute-start | bytes 3145736 | tf_op jit(solution)/shard_map/ppermute | solution.py:193
  6.9 25.2 %collective-permute-start.2 = (bf16[128,4096]{1,0:T(8,128)(2,1)S(1)}, bf16[128,4096]{1,0:T(8,128)(2,1)S(1)}, u32[]{:S(2)}, u32[]{:S(2)}) collective-permute-start(bf16[128,4096]{1,0:T(8,128)(2,1)S(1)} %fusion.2), channel_id=1, source_target_pairs={{0,18},{1,19},{2,16},{3,17},{16,2},{17,3},{18,0},{19,1},{4,22},{5,... | collective-permute-start | bytes 3145736 | tf_op jit(solution)/shard_map/ppermute | solution.py:193
  10.6 21.5 %collective-permute-start.3 = (bf16[256,1024]{1,0:T(8,128)(2,1)}, bf16[256,1024]{1,0:T(8,128)(2,1)}, u32[]{:S(2)}, u32[]{:S(2)}) collective-permute-start(bf16[256,1024]{1,0:T(8,128)(2,1)} %maximum_maximum_fusion), channel_id=1, source_target_pairs={{0,4},{4,0},{8,12},{12,8},{1,5},{5,1},{9,13},{13,9},{2,6},{6,2},{1... | collective-permute-start | bytes 1572872 | tf_op jit(solution)/shard_map/ppermute | solution.py:23
  32.5 15.6 %collective-permute-start.4 = (bf16[256,2048]{1,0:T(8,128)(2,1)S(1)}, bf16[256,2048]{1,0:T(8,128)(2,1)S(1)}, u32[]{:S(2)}, u32[]{:S(2)}) collective-permute-start(bf16[256,2048]{1,0:T(8,128)(2,1)S(1)} %fusion.17), channel_id=1, source_target_pairs={{0,16},{16,0},{1,17},{17,1},{2,18},{18,2},{3,19},{19,3},{4,20},{20... | collective-permute-start | bytes 3145736 | tf_op jit(solution)/shard_map/ppermute | solution.py:23
  32.7 14.2 %collective-permute-start.5 = (bf16[64,4096]{1,0:T(8,128)(2,1)S(1)}, bf16[64,4096]{1,0:T(8,128)(2,1)S(1)}, u32[]{:S(2)}, u32[]{:S(2)}) collective-permute-start(bf16[64,4096]{1,0:T(8,128)(2,1)S(1)} %slice.169), channel_id=1, source_target_pairs={{0,2},{1,3},{2,0},{3,1},{4,6},{5,7},{6,4},{7,5},{8,10},{9,11},{10,... | collective-permute-start | bytes 1572872 | tf_op jit(solution)/shard_map/ppermute | solution.py:23
  34.2 13.9 %collective-permute-start.6 = (bf16[64,4096]{1,0:T(8,128)(2,1)S(1)}, bf16[64,4096]{1,0:T(8,128)(2,1)S(1)}, u32[]{:S(2)}, u32[]{:S(2)}) collective-permute-start(bf16[64,4096]{1,0:T(8,128)(2,1)S(1)} %slice.170), channel_id=1, source_target_pairs={{0,1},{1,0},{2,3},{3,2},{4,5},{5,4},{6,7},{7,6},{8,9},{9,8},{10,11... | collective-permute-start | bytes 1572872 | tf_op jit(solution)/shard_map/ppermute | solution.py:23
  48.1 13.3 %collective-permute-start.7 = (bf16[256,1024]{1,0:T(8,128)(2,1)}, bf16[256,1024]{1,0:T(8,128)(2,1)S(1)}, u32[]{:S(2)}, u32[]{:S(2)}) collective-permute-start(bf16[256,1024]{1,0:T(8,128)(2,1)} %collective-permute-done.3), channel_id=1, source_target_pairs={{0,1},{1,0},{2,3},{3,2},{4,5},{5,4},{6,7},{7,6},{8,9},{9,8},{10,11... | collective-permute-start | bytes 1572872 | tf_op jit(solution)/shard_map/ppermute | solution.py:23
  48.7 13.0 %collective-permute-start.8 = (bf16[256,1024]{1,0:T(8,128)(2,1)}, bf16[256,1024]{1,0:T(8,128)(2,1)S(1)}, u32[]{:S(2)}, u32[]{:S(2)}) collective-permute-start(bf16[256,1024]{1,0:T(8,128)(2,1)} %collective-permute-done.3), channel_id=1, source_target_pairs={{0,2},{1,3},{2,0},{3,1},{4,6},{5,7},{6,4},{7,5},{8,10},{9,11},{10,... | collective-permute-start | bytes 1572872 | tf_op jit(solution)/shard_map/ppermute | solution.py:23
  53.4 16.4 %collective-permute-start.10 = (bf16[512,512]{1,0:T(8,128)(2,1)S(1)}, bf16[512,512]{1,0:T(8,128)(2,1)S(1)}, u32[]{:S(2)}, u32[]{:S(2)}) collective-permute-start(bf16[512,512]{1,0:T(8,128)(2,1)S(1)} %get-tuple-element.280.refs_0_), channel_id=1, source_target_pairs={{0,4},{4,0},{8,12},{12,8},{1,5},{5,1},{9,13},{13,9},{2,6},{6,2},{1... | collective-permute-start | bytes 1572872 | tf_op jit(solution)/shard_map/ppermute | solution.py:23
  55.3 16.2 %collective-permute-start.11 = (bf16[512,512]{1,0:T(8,128)(2,1)S(1)}, bf16[512,512]{1,0:T(8,128)(2,1)S(1)}, u32[]{:S(2)}, u32[]{:S(2)}) collective-permute-start(bf16[512,512]{1,0:T(8,128)(2,1)S(1)} %get-tuple-element.280.refs_0_), channel_id=1, source_target_pairs={{0,16},{16,0},{1,17},{17,1},{2,18},{18,2},{3,19},{19,3},{4,20},{20... | collective-permute-start | bytes 1572872 | tf_op jit(solution)/shard_map/ppermute | solution.py:23
  69.8 18.4 %collective-permute-start.19 = (bf16[512,512]{1,0:T(8,128)(2,1)S(1)}, bf16[512,512]{1,0:T(8,128)(2,1)S(1)}, u32[]{:S(2)}, u32[]{:S(2)}) collective-permute-start(bf16[512,512]{1,0:T(8,128)(2,1)S(1)} %get-tuple-element.277.refs_1_), channel_id=1, source_target_pairs={{0,4},{4,0},{8,12},{12,8},{1,5},{5,1},{9,13},{13,9},{2,6},{6,2},{1... | collective-permute-start | bytes 1572872 | tf_op jit(solution)/shard_map/ppermute | solution.py:23
  77.2 11.1 %collective-permute-start.18 = (bf16[512,512]{1,0:T(8,128)(2,1)S(1)}, bf16[512,512]{1,0:T(8,128)(2,1)S(1)}, u32[]{:S(2)}, u32[]{:S(2)}) collective-permute-start(bf16[512,512]{1,0:T(8,128)(2,1)S(1)} %get-tuple-element.306), channel_id=1, source_target_pairs={{4,8},{8,4},{5,9},{9,5},{6,10},{10,6},{7,11},{11,7},{20,24},{24,20... | collective-permute-start | bytes 1572872 | tf_op jit(solution)/shard_map/ppermute | solution.py:341
  77.9 17.6 %collective-permute-start.21 = (bf16[512,512]{1,0:T(8,128)(2,1)S(1)}, bf16[512,512]{1,0:T(8,128)(2,1)S(1)}, u32[]{:S(2)}, u32[]{:S(2)}) collective-permute-start(bf16[512,512]{1,0:T(8,128)(2,1)S(1)} %get-tuple-element.263.refs_2_), channel_id=1, source_target_pairs={{0,4},{4,0},{8,12},{12,8},{1,5},{5,1},{9,13},{13,9},{2,6},{6,2},{1... | collective-permute-start | bytes 1572872 | tf_op jit(solution)/shard_map/ppermute | solution.py:23
  82.3 26.7 %collective-permute-start.23 = (bf16[512,512]{1,0:T(8,128)(2,1)}, bf16[512,512]{1,0:T(8,128)(2,1)S(1)}, u32[]{:S(2)}, u32[]{:S(2)}) collective-permute-start(bf16[512,512]{1,0:T(8,128)(2,1)} %get-tuple-element.305), channel_id=1, source_target_pairs={{4,8},{8,4},{5,9},{9,5},{6,10},{10,6},{7,11},{11,7},{20,24},{24,20... | collective-permute-start | bytes 1572872 | tf_op jit(solution)/shard_map/ppermute | solution.py:344
  95.5 14.3 %collective-permute-start.22 = (bf16[512,512]{1,0:T(8,128)(2,1)S(1)}, bf16[512,512]{1,0:T(8,128)(2,1)S(1)}, u32[]{:S(2)}, u32[]{:S(2)}) collective-permute-start(bf16[512,512]{1,0:T(8,128)(2,1)S(1)} %collective-permute-done.21), channel_id=1, source_target_pairs={{0,16},{16,0},{1,17},{17,1},{2,18},{18,2},{3,19},{19,3},{4,20},{20... | collective-permute-start | bytes 1572872 | tf_op jit(solution)/shard_map/ppermute | solution.py:23
  96.3 23.3 %collective-permute-start.24 = (bf16[512,512]{1,0:T(8,128)(2,1)}, bf16[512,512]{1,0:T(8,128)(2,1)}, u32[]{:S(2)}, u32[]{:S(2)}) collective-permute-start(bf16[512,512]{1,0:T(8,128)(2,1)} %get-tuple-element.304), channel_id=1, source_target_pairs={{4,8},{8,4},{5,9},{9,5},{6,10},{10,6},{7,11},{11,7},{20,24},{24,20... | collective-permute-start | bytes 1572872 | tf_op jit(solution)/shard_map/ppermute | solution.py:341
  98.0 25.6 %collective-permute-start.25 = (bf16[256,2048]{1,0:T(8,128)(2,1)S(1)}, bf16[256,2048]{1,0:T(8,128)(2,1)S(1)}, u32[]{:S(2)}, u32[]{:S(2)}) collective-permute-start(bf16[256,2048]{1,0:T(8,128)(2,1)S(1)} %pad_maximum_fusion.1), channel_id=1, source_target_pairs={{0,1},{1,0},{2,3},{3,2},{4,5},{5,4},{6,7},{7,6},{8,9},{9,8},{10,11... | collective-permute-start | bytes 3145736 | tf_op jit(solution)/shard_map/ppermute | solution.py:23
  98.6 22.5 %collective-permute-start.26 = (bf16[512,512]{1,0:T(8,128)(2,1)S(1)}, bf16[512,512]{1,0:T(8,128)(2,1)S(1)}, u32[]{:S(2)}, u32[]{:S(2)}) collective-permute-start(bf16[512,512]{1,0:T(8,128)(2,1)S(1)} %get-tuple-element.272.refs_3_), channel_id=1, source_target_pairs={{0,4},{4,0},{8,12},{12,8},{1,5},{5,1},{9,13},{13,9},{2,6},{6,2},{1... | collective-permute-start | bytes 1572872 | tf_op jit(solution)/shard_map/ppermute | solution.py:23
  109.1 18.7 %collective-permute-start.28 = (bf16[512,512]{1,0:T(8,128)(2,1)S(1)}, bf16[512,512]{1,0:T(8,128)(2,1)S(1)}, u32[]{:S(2)}, u32[]{:S(2)}) collective-permute-start(bf16[512,512]{1,0:T(8,128)(2,1)S(1)} %get-tuple-element.303), channel_id=1, source_target_pairs={{4,8},{8,4},{5,9},{9,5},{6,10},{10,6},{7,11},{11,7},{20,24},{24,20... | collective-permute-start | bytes 1572872 | tf_op jit(solution)/shard_map/ppermute | solution.py:344
  109.8 26.3 %collective-permute-start.29 = (bf16[512,512]{1,0:T(8,128)(2,1)}, bf16[512,512]{1,0:T(8,128)(2,1)S(1)}, u32[]{:S(2)}, u32[]{:S(2)}) collective-permute-start(bf16[512,512]{1,0:T(8,128)(2,1)} %fusion.13), channel_id=1, source_target_pairs={{0,4},{4,0},{8,12},{12,8},{1,5},{5,1},{9,13},{13,9},{2,6},{6,2},{1... | collective-permute-start | bytes 1572872 | tf_op jit(solution)/shard_map/ppermute | solution.py:23
  119.6 26.2 %collective-permute-start.32 = (bf16[256,2048]{1,0:T(8,128)(2,1)S(1)}, bf16[256,2048]{1,0:T(8,128)(2,1)S(1)}, u32[]{:S(2)}, u32[]{:S(2)}) collective-permute-start(bf16[256,2048]{1,0:T(8,128)(2,1)S(1)} %concatenate.61), channel_id=1, source_target_pairs={{0,2},{1,3},{2,0},{3,1},{4,6},{5,7},{6,4},{7,5},{8,10},{9,11},{10,... | collective-permute-start | bytes 3145736 | tf_op jit(solution)/shard_map/ppermute | solution.py:23
  123.6 13.1 %collective-permute-start.27 = (bf16[512,512]{1,0:T(8,128)(2,1)S(1)}, bf16[512,512]{1,0:T(8,128)(2,1)S(1)}, u32[]{:S(2)}, u32[]{:S(2)}) collective-permute-start(bf16[512,512]{1,0:T(8,128)(2,1)S(1)} %collective-permute-done.26), channel_id=1, source_target_pairs={{0,16},{16,0},{1,17},{17,1},{2,18},{18,2},{3,19},{19,3},{4,20},{20... | collective-permute-start | bytes 1572872 | tf_op jit(solution)/shard_map/ppermute | solution.py:23
  124.4 21.3 %collective-permute-start.30 = (bf16[512,512]{1,0:T(8,128)(2,1)S(1)}, bf16[512,512]{1,0:T(8,128)(2,1)S(1)}, u32[]{:S(2)}, u32[]{:S(2)}) collective-permute-start(bf16[512,512]{1,0:T(8,128)(2,1)S(1)} %get-tuple-element.302), channel_id=1, source_target_pairs={{4,8},{8,4},{5,9},{9,5},{6,10},{10,6},{7,11},{11,7},{20,24},{24,20... | collective-permute-start | bytes 1572872 | tf_op jit(solution)/shard_map/ppermute | solution.py:341
  127.7 20.6 %collective-permute-start.31 = (bf16[512,512]{1,0:T(8,128)(2,1)S(1)}, bf16[512,512]{1,0:T(8,128)(2,1)S(1)}, u32[]{:S(2)}, u32[]{:S(2)}) collective-permute-start(bf16[512,512]{1,0:T(8,128)(2,1)S(1)} %fusion.14), channel_id=1, source_target_pairs={{0,4},{4,0},{8,12},{12,8},{1,5},{5,1},{9,13},{13,9},{2,6},{6,2},{1... | collective-permute-start | bytes 1572872 | tf_op jit(solution)/shard_map/ppermute | solution.py:23
  136.0 12.4 %collective-permute-start.33 = (bf16[512,512]{1,0:T(8,128)(2,1)S(1)}, bf16[512,512]{1,0:T(8,128)(2,1)S(1)}, u32[]{:S(2)}, u32[]{:S(2)}) collective-permute-start(bf16[512,512]{1,0:T(8,128)(2,1)S(1)} %get-tuple-element.301), channel_id=1, source_target_pairs={{4,8},{8,4},{5,9},{9,5},{6,10},{10,6},{7,11},{11,7},{20,24},{24,20... | collective-permute-start | bytes 1572872 | tf_op jit(solution)/shard_map/ppermute | solution.py:344
  136.7 30.2 %collective-permute-start.36 = (bf16[128,2048]{1,0:T(8,128)(2,1)S(1)}, bf16[128,2048]{1,0:T(8,128)(2,1)S(1)}, u32[]{:S(2)}, u32[]{:S(2)}) collective-permute-start(bf16[128,2048]{1,0:T(8,128)(2,1)S(1)} %add_convert_fusion.7), channel_id=1, source_target_pairs={{0,2},{1,3},{2,0},{3,1},{4,6},{5,7},{6,4},{7,5},{8,10},{9,11},{10,... | collective-permute-start | bytes 1572872 | tf_op jit(solution)/shard_map/ppermute | solution.py:23
  148.5 18.6 %collective-permute-start.37 = (bf16[128,2048]{1,0:T(8,128)(2,1)S(1)}, bf16[128,2048]{1,0:T(8,128)(2,1)S(1)}, u32[]{:S(2)}, u32[]{:S(2)}) collective-permute-start(bf16[128,2048]{1,0:T(8,128)(2,1)S(1)} %add_convert_fusion.5), channel_id=1, source_target_pairs={{0,1},{1,0},{2,3},{3,2},{4,5},{5,4},{6,7},{7,6},{8,9},{9,8},{10,11... | collective-permute-start | bytes 1572872 | tf_op jit(solution)/shard_map/ppermute | solution.py:23
  149.2 22.8 %collective-permute-start.34 = (bf16[512,512]{1,0:T(8,128)(2,1)S(1)}, bf16[512,512]{1,0:T(8,128)(2,1)S(1)}, u32[]{:S(2)}, u32[]{:S(2)}) collective-permute-start(bf16[512,512]{1,0:T(8,128)(2,1)S(1)} %slice.205), channel_id=1, source_target_pairs={{4,8},{8,4},{5,9},{9,5},{6,10},{10,6},{7,11},{11,7},{20,24},{24,20... | collective-permute-start | bytes 1572872 | tf_op jit(solution)/shard_map/ppermute | solution.py:341
  150.8 23.1 %collective-permute-start.35 = (bf16[512,512]{1,0:T(8,128)(2,1)S(1)}, bf16[512,512]{1,0:T(8,128)(2,1)S(1)}, u32[]{:S(2)}, u32[]{:S(2)}) collective-permute-start(bf16[512,512]{1,0:T(8,128)(2,1)S(1)} %fusion.15), channel_id=1, source_target_pairs={{0,4},{4,0},{8,12},{12,8},{1,5},{5,1},{9,13},{13,9},{2,6},{6,2},{1... | collective-permute-start | bytes 1572872 | tf_op jit(solution)/shard_map/ppermute | solution.py:23
  162.6 17.1 %collective-permute-start.39 = (bf16[512,512]{1,0:T(8,128)(2,1)S(1)}, bf16[512,512]{1,0:T(8,128)(2,1)S(1)}, u32[]{:S(2)}, u32[]{:S(2)}) collective-permute-start(bf16[512,512]{1,0:T(8,128)(2,1)S(1)} %slice.216), channel_id=1, source_target_pairs={{4,8},{8,4},{5,9},{9,5},{6,10},{10,6},{7,11},{11,7},{20,24},{24,20... | collective-permute-start | bytes 1572872 | tf_op jit(solution)/shard_map/ppermute | solution.py:344
  167.5 23.9 %collective-permute-start.38 = (bf16[128,4096]{1,0:T(8,128)(2,1)S(1)}, bf16[128,4096]{1,0:T(8,128)(2,1)S(1)}, u32[]{:S(2)}, u32[]{:S(2)}) collective-permute-start(bf16[128,4096]{1,0:T(8,128)(2,1)S(1)} %pad_maximum_fusion.2), channel_id=1, source_target_pairs={{0,16},{16,0},{1,17},{17,1},{2,18},{18,2},{3,19},{19,3},{4,20},{20... | collective-permute-start | bytes 3145736 | tf_op jit(solution)/shard_map/ppermute | solution.py:23
  174.3 16.0 %collective-permute-start.40 = (bf16[512,512]{1,0:T(8,128)(2,1)S(1)}, bf16[512,512]{1,0:T(8,128)(2,1)S(1)}, u32[]{:S(2)}, u32[]{:S(2)}) collective-permute-start(bf16[512,512]{1,0:T(8,128)(2,1)S(1)} %fusion.16), channel_id=1, source_target_pairs={{0,4},{4,0},{8,12},{12,8},{1,5},{5,1},{9,13},{13,9},{2,6},{6,2},{1... | collective-permute-start | bytes 1572872 | tf_op jit(solution)/shard_map/ppermute | solution.py:23
  (20 other events, 114.3 us)
where the time goes:
time: 198 us; the launch traced here: 194 us
  starting transfers between devices  63.3 us (32%)
  waiting for transfers between devices  50 us (25%)
  matrix products  38.7 us (20%)
  Pallas kernels  21.1 us (11%)
  other arithmetic  10.4 us (5%)
  local copies, waits for them, and re-layouts  8.98 us (5%)
    ppermute x31, starting transfers between devices, swap(): return lax.ppermute(value, axis, pairs)  52.9 us
    ppermute x31, waiting for transfers between devices, swap(): return lax.ppermute(value, axis, pairs)  32.2 us
    dot_general x40, matrix products, dot(): lax.dot_general(left, right, (((left_dim,), (right_dim,)), ((), ())), pre...  25.5 us
    ppermute x2, waiting for transfers between devices, swap_both(): return lax.ppermute(rows, ('section', 'seq'), pairs)  17.8 us
    pallas_call x2, Pallas kernels, row_product(): pl.pallas_call(functools.partial(row_kernel, len(grads)), grid=(steps,),...  10.8 us
    dot_general x1, matrix products, on_device(): jnp.dot(early, key_weight, preferred_element_type=F32).astype(BF16)  7.28 us
    pallas_call x4, Pallas kernels, attend_head(): pl.pallas_call(attend_kernel, grid=(1,), in_specs=[whole(src_rows, 1), co...  6.04 us
    pallas_call x4, Pallas kernels, add_columns(): pl.pallas_call(functools.partial(add_kernel, count), grid=(1,), in_specs=...  4.29 us
  transfers between devices with their start and end apart: 41, of which 12 were waited for; matrix products, arithmetic and copies ran while one was open for 26% of the time, Pallas kernels for 11%

commit v1 on v0

--- a/solution.py
+++ b/solution.py
@@ -46,9 +46,8 @@
     )
 
 
-def attend_kernel(
-    visible, query, key_early, key_late, value_early, value_late, upstream, attended, query_grad, kv_grad
-):
+def attend_kernel(visible, query, key_early, key_late, value_early, value_late, upstream, *refs):
+    attended, query_grad, kv_grad = refs[-3:]
     score_scale = HD ** (-0.5)
     query_rows, upstream_rows = query[...], upstream[...]
     key_rows = jnp.concatenate([key_early[...], key_late[...]], axis=0)
@@ -67,7 +66,7 @@
     query_grad[...] = dot(grad_scores, key_rows, 0, 0).astype(BF16)
 
 
-def attend_head(head, visible, query, key_early, key_late, value_early, value_late, upstream):
+def attend_head(head, visible, query, key_early, key_late, value_early, value_late, upstream, kept):
     src_rows, target_rows = visible.shape[0], query.shape[0]
     early, late = key_early.shape[0], key_late.shape[0]
 
@@ -88,16 +87,18 @@
             column(early),
             column(late),
             column(target_rows),
-        ],
-        out_specs=[whole(target_rows, HD), whole(target_rows, HD), whole(src_rows, 2 * HD)],
+        ]
+        + [pl.BlockSpec(memory_space=pl.ANY)] * len(kept),
+        out_specs=[column(target_rows), column(target_rows), whole(src_rows, 2 * HD)],
         out_shape=[
-            jax.ShapeDtypeStruct((target_rows, HD), BF16),
-            jax.ShapeDtypeStruct((target_rows, HD), BF16),
+            jax.ShapeDtypeStruct(query.shape, BF16),
+            jax.ShapeDtypeStruct(query.shape, BF16),
             jax.ShapeDtypeStruct((src_rows, 2 * HD), BF16),
         ],
+        input_output_aliases={7 + slot: slot for slot in range(len(kept))},
         compiler_params=pltpu.CompilerParams(vmem_limit_bytes=6 * MIB + 40 * src_rows * target_rows),
         cost_estimate=FILLS_WAITS,
-    )(visible, query, key_early, key_late, value_early, value_late, upstream)
+    )(visible, query, key_early, key_late, value_early, value_late, upstream, *kept)
 
 
 def row_kernel(head_count, *refs):
@@ -234,9 +235,12 @@
 
     held["key_early"] = key_early
 
+    outputs = []
+
     def attend(head):
-        held[("attended", head)], held[("query", head)], held[("kv", head)] = attend_head(
-            head, visible, queries[0], held["key_early"], key_late, value_early, value_late, out_grad[0]
+        early_keys = held["key_early"]
+        *outputs[:], held[("kv", head)] = attend_head(
+            head, visible, queries[0], early_keys, key_late, value_early, value_late, out_grad[0], list(outputs)
         )
 
     def hand_in(head):
@@ -334,13 +338,12 @@
             *([("relay", 1)] if head == 3 else []),
             "row_low",
             "row_high",
-            *([("row_low", "first")] if head == 2 else [("row_high", "first")] if head == 3 else []),
+            *([("row_high", "first")] if head == 2 else []),
+            *([("row_low", "second"), ("row_high", "second")] if head == 3 else []),
             *kinds("kv", "their"),
             *((("handed", head + 1),) if head > 0 else ()),
         )
         held[("outward", head)] = lax.ppermute(held["far"][:target_width], "dp", across)
-        if head == last:
-            sync("far", ("inner", head - 1), *kinds("attended", "query"))
         held[("inner", head)] = lax.ppermute(held["far"][target_width:], "dp", across)
         hand_in(head + 2)
         if head > 0:
@@ -349,6 +352,10 @@
             if head == 0:
                 grads = [held[("kv", other)] for other in heads]
                 held["row_low"] = row_product(grads, key_weight, value_weight, 0, 2)
+                if by_steps:
+                    first_step("row_low", 1, 3)
+                    held["row_high"] = row_product(grads, key_weight, value_weight, 1, 2)
+                    first_step("row_high", 2, 3)
                 sync(("outward", 0), ("handed", 1), *kinds("their"))
                 held[("near", 1)] = chip_sum("chip_far", 1)
             held[("other", head + 1)] = swap(held[("handed", head + 1)], "section", 1)
@@ -357,40 +364,33 @@
                     ("other", head + 1),
                     ("inner", head - 1),
                     ("relay", head - 2),
+                    *([("row_low", "first")] if head == 1 else []),
                     *kinds("kv", "their"),
                 )
                 held[("near", head + 1)] = chip_sum("chip_far", head + 1)
         if head == 1:
             if by_steps:
-                first_step("row_low", 1, 3)
-            grads = [held[("kv", other)] for other in heads]
-            held["row_high"] = row_product(grads, key_weight, value_weight, 1, 2)
-            if by_steps:
-                first_step("row_high", 2, 3)
-        if head == 2:
-            if by_steps:
                 second_step("row_low", 2)
-        if head == 3:
-            if by_steps:
-                second_step("row_high", 1)
-    if heads_here == 1:
-        held["row_low"] = row_product([held[("kv", 0)]], key_weight, value_weight, 0, 2)
-        held["row_high"] = row_product([held[("kv", 0)]], key_weight, value_weight, 1, 2)
+        if head == 2 and by_steps:
+            second_step("row_high", 1)
+    if not by_steps:
+        held["row_low"] = row_product([held[("kv", head)] for head in heads], key_weight, value_weight, 0, 2)
+        held["row_high"] = row_product([held[("kv", head)] for head in heads], key_weight, value_weight, 1, 2)
+    sync(*kinds("outward", "relay"), *(("inner", head) for head in heads[:-1]), *kinds("kv", "their"))
+    relay(last)
     for head in heads[:-1]:
         finish(head)
-    sync(("outward", last), *(("relay", head) for head in heads[:-1]))
-    relay(last)
-    finish(last)
-
     row_share = jnp.concatenate([row_total("row_low"), row_total("row_high")], axis=1)
     row_grad = swap(row_share.astype(BF16), "section", 1)
-    enc_grad = norm_backward(enc_rows, held["factor"], enc_gain, row_grad)
+    held["enc_grad"] = norm_backward(enc_rows, held["factor"], enc_gain, row_grad)
+    sync(("relay", last), "enc_grad")
+    finish(last)
     return (
-        jnp.concatenate([held[("attended", head)] for head in heads], axis=1)[None],
-        enc_grad[None],
+        outputs[0][None],
+        held["enc_grad"][None],
         held[("total", 0)],
         held[("total", 1)],
-        jnp.concatenate([held[("query", head)] for head in heads], axis=1)[None],
+        outputs[1][None],
     )
 
 

time: 198 us -> 183 us (0.924)
  starting transfers between devices: 63.3 us -> 51.4 us
  Pallas kernels: 21.1 us -> 23.7 us
  local copies, waits for them, and re-layouts: 8.98 us -> 6.78 us
  other arithmetic: 10.4 us -> 8.21 us
    ppermute x31, starting transfers between devices: 52.9 us -> 41.6 us  [swap(): return lax.ppermute(value, axis, pairs)]
    broadcast_in_dim x3 -> x0, other arithmetic: 3.92 us -> none  [the longest x1 1.7 us: on_device(): enc_grad[None]]
    pallas_call x4, Pallas kernels: 6.04 us -> 8.87 us  [attend_head(): pl.pallas_call(attend_kernel, grid=(1,), in_specs=[whole(src_rows, 1), co...]
  transfers between devices with their start and end apart: 41 -> 41, of which waited for: 12 -> 12; matrix products, arithmetic and copies ran while one was open for 26% -> 27% of each run, Pallas kernels for 11% -> 13%
where the time goes in v1:
time: 183 us; the launch traced here: 179 us
  starting transfers between devices  51.4 us (28%)
  waiting for transfers between devices  50.1 us (27%)
  matrix products  37.2 us (20%)
  Pallas kernels  23.7 us (13%)
  other arithmetic  8.21 us (4%)
  local copies, waits for them, and re-layouts  6.78 us (4%)
    ppermute x31, starting transfers between devices, swap(): return lax.ppermute(value, axis, pairs)  41.6 us
    ppermute x31, waiting for transfers between devices, swap(): return lax.ppermute(value, axis, pairs)  32.3 us
    dot_general x40, matrix products, dot(): lax.dot_general(left, right, (((left_dim,), (right_dim,)), ((), ())), pre...  24 us
    ppermute x2, waiting for transfers between devices, swap_both(): return lax.ppermute(rows, ('section', 'seq'), pairs)  17.8 us
    pallas_call x2, Pallas kernels, row_product(): pl.pallas_call(functools.partial(row_kernel, len(grads)), grid=(steps,),...  10.5 us
    pallas_call x4, Pallas kernels, attend_head(): pl.pallas_call(attend_kernel, grid=(1,), in_specs=[whole(src_rows, 1), co...  8.87 us
    dot_general x1, matrix products, on_device(): jnp.dot(early, key_weight, preferred_element_type=F32).astype(BF16)  7.28 us
    pallas_call x4, Pallas kernels, add_columns(): pl.pallas_call(functools.partial(add_kernel, count), grid=(1,), in_specs=...  4.26 us
  transfers between devices with their start and end apart: 41, of which 12 were waited for; matrix products, arithmetic and copies ran while one was open for 27% of the time, Pallas kernels for 13%

profile of v1, /device:TPU:0, one launch (start us, length us, event | category | flops | bytes accessed | tf_op | source)
XLA Modules:
  0.0 179.0 jit_solution(10801155495541021982)
XLA Ops:
  0.6 1.5 fusion
  2.2 1.6 fusion.2
  4.3 2.6 %collective-permute-start.1 = (bf16[128,4096]{1,0:T(8,128)(2,1)S(1)}, bf16[128,4096]{1,0:T(8,128)(2,1)S(1)}, u32[]{:S(2)}, u32[]{:S(2)}) collective-permute-start(bf16[128,4096]{1,0:T(8,128)(2,1)S(1)} %fusion.2), channel_id=1, source_target_pairs={{0,17},{1,16},{2,19},{3,18},{16,1},{17,0},{18,3},{19,2},{4,21},{5,... | collective-permute-start | bytes 3145736 | tf_op jit(solution)/shard_map/ppermute | solution.py:194
  10.6 1.6 collective-permute-start.3
  14.3 16.0 %collective-permute-done.1 = bf16[128,4096]{1,0:T(8,128)(2,1)S(1)} collective-permute-done((bf16[128,4096]{1,0:T(8,128)(2,1)S(1)}, bf16[128,4096]{1,0:T(8,128)(2,1)S(1)}, u32[]{:S(2)}, u32[]{:S(2)}) %collective-permute-start.1) | collective-permute-done | bytes 1048608 | tf_op jit(solution)/shard_map/ppermute | solution.py:194
  30.3 1.8 collective-permute-done.2
  32.7 1.6 collective-permute-start.5
  34.8 7.3 %convolution_convert_fusion.1.key_early = bf16[384,1024]{1,0:T(8,128)(2,1)S(1)} fusion(bf16[384,4096]{1,0:T(8,128)(2,1)S(1)} %constant_dynamic-update-slice_fusion, bf16[4096,1024]{1,0:T(8,128)(2,1)} %refs_4_.3), kind=kOutput, calls=%fused_computation.27 | convolution fusion | flops 3221618688 | bytes 12320768 | tf_op jit(solution)/shard_map/dot_general | solution.py:222
  42.1 3.4 %convolution_convert_fusion.value_early = bf16[384,1024]{1,0:T(8,128)(2,1)S(1)} fusion(bf16[384,4096]{1,0:T(8,128)(2,1)S(1)} %constant_dynamic-update-slice_fusion, bf16[4096,1024]{1,0:T(8,128)(2,1)S(1)} %bitcast.67), kind=kOutput, calls=%fused_computation.26 | convolution fusion | flops 3221618688 | bytes 12320768 | tf_op jit(solution)/shard_map/dot_general | solution.py:221
  52.0 2.2 %shard_map.110 = (bf16[512,1024]{1,0:T(8,128)(2,1)}, bf16[512,1024]{1,0:T(8,128)(2,1)}, bf16[512,512]{1,0:T(8,128)(2,1)S(1)}) custom-call(s32[512,1]{1,0:T(8,128)S(1)} %copy.27.visible, bf16[512,1024]{1,0:T(8,128)(2,1)S(1)} %bitcast.68, bf16[384,1024]{1,0:T(8,128)(2,1)S(1)} %convolution_convert_fusion.1.key_early, ...), custom_call_target="tpu_custom_call" | custom-call | tf_op jit(solution)/shard_map/pallas_call | solution.py:79
  54.2 1.8 %collective-permute-start.10 = (bf16[512,512]{1,0:T(8,128)(2,1)S(1)}, bf16[512,512]{1,0:T(8,128)(2,1)S(1)}, u32[]{:S(2)}, u32[]{:S(2)}) collective-permute-start(bf16[512,512]{1,0:T(8,128)(2,1)S(1)} %get-tuple-element.298.refs_0_), channel_id=1, source_target_pairs={{0,4},{4,0},{8,12},{12,8},{1,5},{5,1},{9,13},{13,9},{2,6},{6,2},{1... | collective-permute-start | bytes 1572872 | tf_op jit(solution)/shard_map/ppermute | solution.py:23
  57.0 4.4 %collective-permute-done.7 = bf16[256,1024]{1,0:T(8,128)(2,1)S(1)} collective-permute-done((bf16[256,1024]{1,0:T(8,128)(2,1)}, bf16[256,1024]{1,0:T(8,128)(2,1)S(1)}, u32[]{:S(2)}, u32[]{:S(2)}) %collective-permute-start.7) | collective-permute-done | bytes 524320 | tf_op jit(solution)/shard_map/ppermute | solution.py:23
  62.4 1.6 collective-permute-start.13
  65.1 2.2 %shard_map.111 = (bf16[512,1024]{1,0:T(8,128)(2,1)}, bf16[512,1024]{1,0:T(8,128)(2,1)}, bf16[512,512]{1,0:T(8,128)(2,1)S(1)}) custom-call(s32[512,1]{1,0:T(8,128)S(1)} %copy.27.visible, bf16[512,1024]{1,0:T(8,128)(2,1)S(1)} %bitcast.69, bf16[384,1024]{1,0:T(8,128)(2,1)S(1)} %convolution_convert_fusion.1.key_early, ...), custom_call_target="tpu_custom_call", output_to_operand_aliasing={{0}: (7, {}), {1}: (8, {})} | custom-call | tf_op jit(solution)/shard_map/pallas_call | solution.py:79
  67.2 2.2 %shard_map.112 = (bf16[512,1024]{1,0:T(8,128)(2,1)}, bf16[512,1024]{1,0:T(8,128)(2,1)}, bf16[512,512]{1,0:T(8,128)(2,1)S(1)}) custom-call(s32[512,1]{1,0:T(8,128)S(1)} %copy.27.visible, bf16[512,1024]{1,0:T(8,128)(2,1)S(1)} %bitcast.70, bf16[384,1024]{1,0:T(8,128)(2,1)S(1)} %convolution_convert_fusion.1.key_early, ...), custom_call_target="tpu_custom_call", output_to_operand_aliasing={{0}: (7, {}), {1}: (8, {})} | custom-call | tf_op jit(solution)/shard_map/pallas_call | solution.py:79
  69.4 2.4 %shard_map.113 = (bf16[512,1024]{1,0:T(8,128)(2,1)}, bf16[512,1024]{1,0:T(8,128)(2,1)}, bf16[512,512]{1,0:T(8,128)(2,1)S(1)}) custom-call(s32[512,1]{1,0:T(8,128)S(1)} %copy.27.visible, bf16[512,1024]{1,0:T(8,128)(2,1)S(1)} %bitcast.71, bf16[384,1024]{1,0:T(8,128)(2,1)S(1)} %convolution_convert_fusion.1.key_early, ...), custom_call_target="tpu_custom_call", output_to_operand_aliasing={{0}: (7, {}), {1}: (8, {})} | custom-call | tf_op jit(solution)/shard_map/pallas_call | solution.py:79
  71.9 1.6 collective-permute-start.19
  79.3 4.4 %collective-permute-start.21 = (bf16[512,512]{1,0:T(8,128)(2,1)S(1)}, bf16[512,512]{1,0:T(8,128)(2,1)S(1)}, u32[]{:S(2)}, u32[]{:S(2)}) collective-permute-start(bf16[512,512]{1,0:T(8,128)(2,1)S(1)} %get-tuple-element.290.refs_2_), channel_id=1, source_target_pairs={{0,4},{4,0},{8,12},{12,8},{1,5},{5,1},{9,13},{13,9},{2,6},{6,2},{1... | collective-permute-start | bytes 1572872 | tf_op jit(solution)/shard_map/ppermute | solution.py:23
  84.4 5.3 %shard_map.114 = bf16[512,2048]{1,0:T(8,128)(2,1)S(1)} custom-call(bf16[512,512]{1,0:T(8,128)(2,1)S(1)} %get-tuple-element.298.refs_0_, bf16[512,512]{1,0:T(8,128)(2,1)S(1)} %get-tuple-element.294.refs_1_, bf16[512,512]{1,0:T(8,128)(2,1)S(1)} %get-tuple-element.290.refs_2_, bf16[512,512]{1,0:T(8,128)(2,1)S(1)} %get-tuple-element.280.refs_3_, ...), custom_call_target="tpu_custom_call" | custom-call | flops 4294967296 | bytes 11534336 | tf_op jit(solution)/shard_map/pallas_call | solution.py:119
  90.5 5.2 %shard_map.115 = bf16[512,2048]{1,0:T(8,128)(2,1)S(1)} custom-call(bf16[512,512]{1,0:T(8,128)(2,1)S(1)} %get-tuple-element.298.refs_0_, bf16[512,512]{1,0:T(8,128)(2,1)S(1)} %get-tuple-element.294.refs_1_, bf16[512,512]{1,0:T(8,128)(2,1)S(1)} %get-tuple-element.290.refs_2_, bf16[512,512]{1,0:T(8,128)(2,1)S(1)} %get-tuple-element.280.refs_3_, ...), custom_call_target="tpu_custom_call" | custom-call | flops 4294967296 | bytes 11534336 | tf_op jit(solution)/shard_map/pallas_call | solution.py:119
  105.1 4.5 %collective-permute-start.27 = (bf16[512,512]{1,0:T(8,128)(2,1)S(1)}, bf16[512,512]{1,0:T(8,128)(2,1)S(1)}, u32[]{:S(2)}, u32[]{:S(2)}) collective-permute-start(bf16[512,512]{1,0:T(8,128)(2,1)S(1)} %get-tuple-element.280.refs_3_), channel_id=1, source_target_pairs={{0,4},{4,0},{8,12},{12,8},{1,5},{5,1},{9,13},{13,9},{2,6},{6,2},{1... | collective-permute-start | bytes 1572872 | tf_op jit(solution)/shard_map/ppermute | solution.py:23
  109.6 5.1 %collective-permute-done.24 = bf16[256,2048]{1,0:T(8,128)(2,1)S(1)} collective-permute-done((bf16[256,2048]{1,0:T(8,128)(2,1)S(1)}, bf16[256,2048]{1,0:T(8,128)(2,1)S(1)}, u32[]{:S(2)}, u32[]{:S(2)}) %collective-permute-start.24) | collective-permute-done | bytes 1048608 | tf_op jit(solution)/shard_map/ppermute | solution.py:23
  115.6 4.6 %collective-permute-start.30 = (bf16[512,512]{1,0:T(8,128)(2,1)S(1)}, bf16[512,512]{1,0:T(8,128)(2,1)S(1)}, u32[]{:S(2)}, u32[]{:S(2)}) collective-permute-start(bf16[512,512]{1,0:T(8,128)(2,1)S(1)} %fusion.13), channel_id=1, source_target_pairs={{0,4},{4,0},{8,12},{12,8},{1,5},{5,1},{9,13},{13,9},{2,6},{6,2},{1... | collective-permute-start | bytes 1572872 | tf_op jit(solution)/shard_map/ppermute | solution.py:23
  126.1 2.5 %collective-permute-start.32 = (bf16[512,512]{1,0:T(8,128)(2,1)S(1)}, bf16[512,512]{1,0:T(8,128)(2,1)S(1)}, u32[]{:S(2)}, u32[]{:S(2)}) collective-permute-start(bf16[512,512]{1,0:T(8,128)(2,1)S(1)} %fusion.14), channel_id=1, source_target_pairs={{0,4},{4,0},{8,12},{12,8},{1,5},{5,1},{9,13},{13,9},{2,6},{6,2},{1... | collective-permute-start | bytes 1572872 | tf_op jit(solution)/shard_map/ppermute | solution.py:23
  129.7 3.9 %collective-permute-done.30.second = bf16[512,512]{1,0:T(8,128)(2,1)S(1)} collective-permute-done((bf16[512,512]{1,0:T(8,128)(2,1)S(1)}, bf16[512,512]{1,0:T(8,128)(2,1)S(1)}, u32[]{:S(2)}, u32[]{:S(2)}) %collective-permute-start.30) | collective-permute-done | bytes 524320 | tf_op jit(solution)/shard_map/ppermute | solution.py:23
  138.8 5.1 %collective-permute-done.32.second = bf16[512,512]{1,0:T(8,128)(2,1)S(1)} collective-permute-done((bf16[512,512]{1,0:T(8,128)(2,1)S(1)}, bf16[512,512]{1,0:T(8,128)(2,1)S(1)}, u32[]{:S(2)}, u32[]{:S(2)}) %collective-permute-start.32) | collective-permute-done | bytes 524320 | tf_op jit(solution)/shard_map/ppermute | solution.py:23
  143.9 1.8 collective-permute-done.34
  147.4 3.3 %collective-permute-start.36 = (bf16[512,512]{1,0:T(8,128)(2,1)S(1)}, bf16[512,512]{1,0:T(8,128)(2,1)S(1)}, u32[]{:S(2)}, u32[]{:S(2)}) collective-permute-start(bf16[512,512]{1,0:T(8,128)(2,1)S(1)} %fusion.15), channel_id=1, source_target_pairs={{0,4},{4,0},{8,12},{12,8},{1,5},{5,1},{9,13},{13,9},{2,6},{6,2},{1... | collective-permute-start | bytes 1572872 | tf_op jit(solution)/shard_map/ppermute | solution.py:23
  152.3 7.6 %collective-permute-done.36.second = bf16[512,512]{1,0:T(8,128)(2,1)S(1)} collective-permute-done((bf16[512,512]{1,0:T(8,128)(2,1)S(1)}, bf16[512,512]{1,0:T(8,128)(2,1)S(1)}, u32[]{:S(2)}, u32[]{:S(2)}) %collective-permute-start.36) | collective-permute-done | bytes 524320 | tf_op jit(solution)/shard_map/ppermute | solution.py:23
  160.9 5.4 %collective-permute-start.38 = (bf16[512,512]{1,0:T(8,128)(2,1)S(1)}, bf16[512,512]{1,0:T(8,128)(2,1)S(1)}, u32[]{:S(2)}, u32[]{:S(2)}) collective-permute-start(bf16[512,512]{1,0:T(8,128)(2,1)S(1)} %fusion.16), channel_id=1, source_target_pairs={{0,4},{4,0},{8,12},{12,8},{1,5},{5,1},{9,13},{13,9},{2,6},{6,2},{1... | collective-permute-start | bytes 1572872 | tf_op jit(solution)/shard_map/ppermute | solution.py:23
  174.4 1.7 fusion.7
  176.1 1.6 collective-permute-done.38.second
  (168 shorter events, 59.7 us)
Async XLA Ops:
  4.3 26.1 %collective-permute-start.1 = (bf16[128,4096]{1,0:T(8,128)(2,1)S(1)}, bf16[128,4096]{1,0:T(8,128)(2,1)S(1)}, u32[]{:S(2)}, u32[]{:S(2)}) collective-permute-start(bf16[128,4096]{1,0:T(8,128)(2,1)S(1)} %fusion.2), channel_id=1, source_target_pairs={{0,17},{1,16},{2,19},{3,18},{16,1},{17,0},{18,3},{19,2},{4,21},{5,... | collective-permute-start | bytes 3145736 | tf_op jit(solution)/shard_map/ppermute | solution.py:194
  6.9 25.2 %collective-permute-start.2 = (bf16[128,4096]{1,0:T(8,128)(2,1)S(1)}, bf16[128,4096]{1,0:T(8,128)(2,1)S(1)}, u32[]{:S(2)}, u32[]{:S(2)}) collective-permute-start(bf16[128,4096]{1,0:T(8,128)(2,1)S(1)} %fusion.2), channel_id=1, source_target_pairs={{0,18},{1,19},{2,16},{3,17},{16,2},{17,3},{18,0},{19,1},{4,22},{5,... | collective-permute-start | bytes 3145736 | tf_op jit(solution)/shard_map/ppermute | solution.py:194
  10.6 21.5 %collective-permute-start.3 = (bf16[256,1024]{1,0:T(8,128)(2,1)}, bf16[256,1024]{1,0:T(8,128)(2,1)}, u32[]{:S(2)}, u32[]{:S(2)}) collective-permute-start(bf16[256,1024]{1,0:T(8,128)(2,1)} %maximum_maximum_fusion), channel_id=1, source_target_pairs={{0,4},{4,0},{8,12},{12,8},{1,5},{5,1},{9,13},{13,9},{2,6},{6,2},{1... | collective-permute-start | bytes 1572872 | tf_op jit(solution)/shard_map/ppermute | solution.py:23
  32.5 15.6 %collective-permute-start.4 = (bf16[256,2048]{1,0:T(8,128)(2,1)S(1)}, bf16[256,2048]{1,0:T(8,128)(2,1)S(1)}, u32[]{:S(2)}, u32[]{:S(2)}) collective-permute-start(bf16[256,2048]{1,0:T(8,128)(2,1)S(1)} %fusion.17), channel_id=1, source_target_pairs={{0,16},{16,0},{1,17},{17,1},{2,18},{18,2},{3,19},{19,3},{4,20},{20... | collective-permute-start | bytes 3145736 | tf_op jit(solution)/shard_map/ppermute | solution.py:23
  32.7 14.2 %collective-permute-start.5 = (bf16[64,4096]{1,0:T(8,128)(2,1)S(1)}, bf16[64,4096]{1,0:T(8,128)(2,1)S(1)}, u32[]{:S(2)}, u32[]{:S(2)}) collective-permute-start(bf16[64,4096]{1,0:T(8,128)(2,1)S(1)} %slice.169), channel_id=1, source_target_pairs={{0,2},{1,3},{2,0},{3,1},{4,6},{5,7},{6,4},{7,5},{8,10},{9,11},{10,... | collective-permute-start | bytes 1572872 | tf_op jit(solution)/shard_map/ppermute | solution.py:23
  34.2 13.9 %collective-permute-start.6 = (bf16[64,4096]{1,0:T(8,128)(2,1)S(1)}, bf16[64,4096]{1,0:T(8,128)(2,1)S(1)}, u32[]{:S(2)}, u32[]{:S(2)}) collective-permute-start(bf16[64,4096]{1,0:T(8,128)(2,1)S(1)} %slice.170), channel_id=1, source_target_pairs={{0,1},{1,0},{2,3},{3,2},{4,5},{5,4},{6,7},{7,6},{8,9},{9,8},{10,11... | collective-permute-start | bytes 1572872 | tf_op jit(solution)/shard_map/ppermute | solution.py:23
  48.2 13.3 %collective-permute-start.7 = (bf16[256,1024]{1,0:T(8,128)(2,1)}, bf16[256,1024]{1,0:T(8,128)(2,1)S(1)}, u32[]{:S(2)}, u32[]{:S(2)}) collective-permute-start(bf16[256,1024]{1,0:T(8,128)(2,1)} %collective-permute-done.3), channel_id=1, source_target_pairs={{0,1},{1,0},{2,3},{3,2},{4,5},{5,4},{6,7},{7,6},{8,9},{9,8},{10,11... | collective-permute-start | bytes 1572872 | tf_op jit(solution)/shard_map/ppermute | solution.py:23
  48.7 13.0 %collective-permute-start.8 = (bf16[256,1024]{1,0:T(8,128)(2,1)}, bf16[256,1024]{1,0:T(8,128)(2,1)S(1)}, u32[]{:S(2)}, u32[]{:S(2)}) collective-permute-start(bf16[256,1024]{1,0:T(8,128)(2,1)} %collective-permute-done.3), channel_id=1, source_target_pairs={{0,2},{1,3},{2,0},{3,1},{4,6},{5,7},{6,4},{7,5},{8,10},{9,11},{10,... | collective-permute-start | bytes 1572872 | tf_op jit(solution)/shard_map/ppermute | solution.py:23
  54.2 17.7 %collective-permute-start.10 = (bf16[512,512]{1,0:T(8,128)(2,1)S(1)}, bf16[512,512]{1,0:T(8,128)(2,1)S(1)}, u32[]{:S(2)}, u32[]{:S(2)}) collective-permute-start(bf16[512,512]{1,0:T(8,128)(2,1)S(1)} %get-tuple-element.298.refs_0_), channel_id=1, source_target_pairs={{0,4},{4,0},{8,12},{12,8},{1,5},{5,1},{9,13},{13,9},{2,6},{6,2},{1... | collective-permute-start | bytes 1572872 | tf_op jit(solution)/shard_map/ppermute | solution.py:23
  56.0 17.6 %collective-permute-start.11 = (bf16[512,512]{1,0:T(8,128)(2,1)S(1)}, bf16[512,512]{1,0:T(8,128)(2,1)S(1)}, u32[]{:S(2)}, u32[]{:S(2)}) collective-permute-start(bf16[512,512]{1,0:T(8,128)(2,1)S(1)} %get-tuple-element.298.refs_0_), channel_id=1, source_target_pairs={{0,16},{16,0},{1,17},{17,1},{2,18},{18,2},{3,19},{19,3},{4,20},{20... | collective-permute-start | bytes 1572872 | tf_op jit(solution)/shard_map/ppermute | solution.py:23
  61.7 12.1 %collective-permute-start.12 = (bf16[128,1024]{1,0:T(8,128)(2,1)S(1)}, bf16[128,1024]{1,0:T(8,128)(2,1)S(1)}, u32[]{:S(2)}, u32[]{:S(2)}) collective-permute-start(bf16[128,1024]{1,0:T(8,128)(2,1)S(1)} %get-tuple-element.334), channel_id=1, source_target_pairs={{0,2},{1,3},{2,0},{3,1},{4,6},{5,7},{6,4},{7,5},{8,10},{9,11},{10,... | collective-permute-start | bytes 786440 | tf_op jit(solution)/shard_map/ppermute | solution.py:23
  71.9 23.9 %collective-permute-start.19 = (bf16[512,512]{1,0:T(8,128)(2,1)S(1)}, bf16[512,512]{1,0:T(8,128)(2,1)S(1)}, u32[]{:S(2)}, u32[]{:S(2)}) collective-permute-start(bf16[512,512]{1,0:T(8,128)(2,1)S(1)} %get-tuple-element.294.refs_1_), channel_id=1, source_target_pairs={{0,4},{4,0},{8,12},{12,8},{1,5},{5,1},{9,13},{13,9},{2,6},{6,2},{1... | collective-permute-start | bytes 1572872 | tf_op jit(solution)/shard_map/ppermute | solution.py:23
  78.6 18.7 %collective-permute-start.18 = (bf16[512,512]{1,0:T(8,128)(2,1)S(1)}, bf16[512,512]{1,0:T(8,128)(2,1)S(1)}, u32[]{:S(2)}, u32[]{:S(2)}) collective-permute-start(bf16[512,512]{1,0:T(8,128)(2,1)S(1)} %get-tuple-element.324), channel_id=1, source_target_pairs={{4,8},{8,4},{5,9},{9,5},{6,10},{10,6},{7,11},{11,7},{20,24},{24,20... | collective-permute-start | bytes 1572872 | tf_op jit(solution)/shard_map/ppermute | solution.py:346
  79.3 22.3 %collective-permute-start.21 = (bf16[512,512]{1,0:T(8,128)(2,1)S(1)}, bf16[512,512]{1,0:T(8,128)(2,1)S(1)}, u32[]{:S(2)}, u32[]{:S(2)}) collective-permute-start(bf16[512,512]{1,0:T(8,128)(2,1)S(1)} %get-tuple-element.290.refs_2_), channel_id=1, source_target_pairs={{0,4},{4,0},{8,12},{12,8},{1,5},{5,1},{9,13},{13,9},{2,6},{6,2},{1... | collective-permute-start | bytes 1572872 | tf_op jit(solution)/shard_map/ppermute | solution.py:23
  83.7 21.3 %collective-permute-start.23 = (bf16[512,512]{1,0:T(8,128)(2,1)S(1)}, bf16[512,512]{1,0:T(8,128)(2,1)S(1)}, u32[]{:S(2)}, u32[]{:S(2)}) collective-permute-start(bf16[512,512]{1,0:T(8,128)(2,1)S(1)} %get-tuple-element.323), channel_id=1, source_target_pairs={{4,8},{8,4},{5,9},{9,5},{6,10},{10,6},{7,11},{11,7},{20,24},{24,20... | collective-permute-start | bytes 1572872 | tf_op jit(solution)/shard_map/ppermute | solution.py:347
  89.9 24.9 %collective-permute-start.24 = (bf16[256,2048]{1,0:T(8,128)(2,1)S(1)}, bf16[256,2048]{1,0:T(8,128)(2,1)S(1)}, u32[]{:S(2)}, u32[]{:S(2)}) collective-permute-start(bf16[256,2048]{1,0:T(8,128)(2,1)S(1)} %pad_maximum_fusion.1), channel_id=1, source_target_pairs={{0,1},{1,0},{2,3},{3,2},{4,5},{5,4},{6,7},{7,6},{8,9},{9,8},{10,11... | collective-permute-start | bytes 3145736 | tf_op jit(solution)/shard_map/ppermute | solution.py:23
  95.8 27.3 %collective-permute-start.26 = (bf16[256,2048]{1,0:T(8,128)(2,1)S(1)}, bf16[256,2048]{1,0:T(8,128)(2,1)S(1)}, u32[]{:S(2)}, u32[]{:S(2)}) collective-permute-start(bf16[256,2048]{1,0:T(8,128)(2,1)S(1)} %concatenate.53), channel_id=1, source_target_pairs={{0,2},{1,3},{2,0},{3,1},{4,6},{5,7},{6,4},{7,5},{8,10},{9,11},{10,... | collective-permute-start | bytes 3145736 | tf_op jit(solution)/shard_map/ppermute | solution.py:23
  101.6 14.1 %collective-permute-start.22 = (bf16[512,512]{1,0:T(8,128)(2,1)S(1)}, bf16[512,512]{1,0:T(8,128)(2,1)S(1)}, u32[]{:S(2)}, u32[]{:S(2)}) collective-permute-start(bf16[512,512]{1,0:T(8,128)(2,1)S(1)} %collective-permute-done.21), channel_id=1, source_target_pairs={{0,16},{16,0},{1,17},{17,1},{2,18},{18,2},{3,19},{19,3},{4,20},{20... | collective-permute-start | bytes 1572872 | tf_op jit(solution)/shard_map/ppermute | solution.py:23
  102.2 20.9 %collective-permute-start.25 = (bf16[512,512]{1,0:T(8,128)(2,1)S(1)}, bf16[512,512]{1,0:T(8,128)(2,1)S(1)}, u32[]{:S(2)}, u32[]{:S(2)}) collective-permute-start(bf16[512,512]{1,0:T(8,128)(2,1)S(1)} %get-tuple-element.322), channel_id=1, source_target_pairs={{4,8},{8,4},{5,9},{9,5},{6,10},{10,6},{7,11},{11,7},{20,24},{24,20... | collective-permute-start | bytes 1572872 | tf_op jit(solution)/shard_map/ppermute | solution.py:346
  105.1 18.1 %collective-permute-start.27 = (bf16[512,512]{1,0:T(8,128)(2,1)S(1)}, bf16[512,512]{1,0:T(8,128)(2,1)S(1)}, u32[]{:S(2)}, u32[]{:S(2)}) collective-permute-start(bf16[512,512]{1,0:T(8,128)(2,1)S(1)} %get-tuple-element.280.refs_3_), channel_id=1, source_target_pairs={{0,4},{4,0},{8,12},{12,8},{1,5},{5,1},{9,13},{13,9},{2,6},{6,2},{1... | collective-permute-start | bytes 1572872 | tf_op jit(solution)/shard_map/ppermute | solution.py:23
  114.7 14.2 %collective-permute-start.29 = (bf16[512,512]{1,0:T(8,128)(2,1)S(1)}, bf16[512,512]{1,0:T(8,128)(2,1)S(1)}, u32[]{:S(2)}, u32[]{:S(2)}) collective-permute-start(bf16[512,512]{1,0:T(8,128)(2,1)S(1)} %get-tuple-element.321), channel_id=1, source_target_pairs={{4,8},{8,4},{5,9},{9,5},{6,10},{10,6},{7,11},{11,7},{20,24},{24,20... | collective-permute-start | bytes 1572872 | tf_op jit(solution)/shard_map/ppermute | solution.py:347
  115.6 18.0 %collective-permute-start.30 = (bf16[512,512]{1,0:T(8,128)(2,1)S(1)}, bf16[512,512]{1,0:T(8,128)(2,1)S(1)}, u32[]{:S(2)}, u32[]{:S(2)}) collective-permute-start(bf16[512,512]{1,0:T(8,128)(2,1)S(1)} %fusion.13), channel_id=1, source_target_pairs={{0,4},{4,0},{8,12},{12,8},{1,5},{5,1},{9,13},{13,9},{2,6},{6,2},{1... | collective-permute-start | bytes 1572872 | tf_op jit(solution)/shard_map/ppermute | solution.py:23
  123.1 12.0 %collective-permute-start.28 = (bf16[512,512]{1,0:T(8,128)(2,1)S(1)}, bf16[512,512]{1,0:T(8,128)(2,1)S(1)}, u32[]{:S(2)}, u32[]{:S(2)}) collective-permute-start(bf16[512,512]{1,0:T(8,128)(2,1)S(1)} %collective-permute-done.27), channel_id=1, source_target_pairs={{0,16},{16,0},{1,17},{17,1},{2,18},{18,2},{3,19},{19,3},{4,20},{20... | collective-permute-start | bytes 1572872 | tf_op jit(solution)/shard_map/ppermute | solution.py:23
  124.5 14.3 %collective-permute-start.31 = (bf16[512,512]{1,0:T(8,128)(2,1)S(1)}, bf16[512,512]{1,0:T(8,128)(2,1)S(1)}, u32[]{:S(2)}, u32[]{:S(2)}) collective-permute-start(bf16[512,512]{1,0:T(8,128)(2,1)S(1)} %get-tuple-element.320), channel_id=1, source_target_pairs={{4,8},{8,4},{5,9},{9,5},{6,10},{10,6},{7,11},{11,7},{20,24},{24,20... | collective-permute-start | bytes 1572872 | tf_op jit(solution)/shard_map/ppermute | solution.py:346
  126.1 17.8 %collective-permute-start.32 = (bf16[512,512]{1,0:T(8,128)(2,1)S(1)}, bf16[512,512]{1,0:T(8,128)(2,1)S(1)}, u32[]{:S(2)}, u32[]{:S(2)}) collective-permute-start(bf16[512,512]{1,0:T(8,128)(2,1)S(1)} %fusion.14), channel_id=1, source_target_pairs={{0,4},{4,0},{8,12},{12,8},{1,5},{5,1},{9,13},{13,9},{2,6},{6,2},{1... | collective-permute-start | bytes 1572872 | tf_op jit(solution)/shard_map/ppermute | solution.py:23
  128.9 15.0 %collective-permute-start.33 = (bf16[128,2048]{1,0:T(8,128)(2,1)S(1)}, bf16[128,2048]{1,0:T(8,128)(2,1)S(1)}, u32[]{:S(2)}, u32[]{:S(2)}) collective-permute-start(bf16[128,2048]{1,0:T(8,128)(2,1)S(1)} %add_convert_fusion.7), channel_id=1, source_target_pairs={{0,2},{1,3},{2,0},{3,1},{4,6},{5,7},{6,4},{7,5},{8,10},{9,11},{10,... | collective-permute-start | bytes 1572872 | tf_op jit(solution)/shard_map/ppermute | solution.py:23
  133.6 12.1 %collective-permute-start.34 = (bf16[128,2048]{1,0:T(8,128)(2,1)S(1)}, bf16[128,2048]{1,0:T(8,128)(2,1)S(1)}, u32[]{:S(2)}, u32[]{:S(2)}) collective-permute-start(bf16[128,2048]{1,0:T(8,128)(2,1)S(1)} %add_convert_fusion.6), channel_id=1, source_target_pairs={{0,1},{1,0},{2,3},{3,2},{4,5},{5,4},{6,7},{7,6},{8,9},{9,8},{10,11... | collective-permute-start | bytes 1572872 | tf_op jit(solution)/shard_map/ppermute | solution.py:23
  135.1 17.2 %collective-permute-start.37 = (bf16[512,512]{1,0:T(8,128)(2,1)S(1)}, bf16[512,512]{1,0:T(8,128)(2,1)S(1)}, u32[]{:S(2)}, u32[]{:S(2)}) collective-permute-start(bf16[512,512]{1,0:T(8,128)(2,1)S(1)} %get-tuple-element.319), channel_id=1, source_target_pairs={{4,8},{8,4},{5,9},{9,5},{6,10},{10,6},{7,11},{11,7},{20,24},{24,20... | collective-permute-start | bytes 1572872 | tf_op jit(solution)/shard_map/ppermute | solution.py:347
  147.4 12.5 %collective-permute-start.36 = (bf16[512,512]{1,0:T(8,128)(2,1)S(1)}, bf16[512,512]{1,0:T(8,128)(2,1)S(1)}, u32[]{:S(2)}, u32[]{:S(2)}) collective-permute-start(bf16[512,512]{1,0:T(8,128)(2,1)S(1)} %fusion.15), channel_id=1, source_target_pairs={{0,4},{4,0},{8,12},{12,8},{1,5},{5,1},{9,13},{13,9},{2,6},{6,2},{1... | collective-permute-start | bytes 1572872 | tf_op jit(solution)/shard_map/ppermute | solution.py:23
  151.3 22.0 %collective-permute-start.39 = (bf16[128,4096]{1,0:T(8,128)(2,1)S(1)}, bf16[128,4096]{1,0:T(8,128)(2,1)S(1)}, u32[]{:S(2)}, u32[]{:S(2)}) collective-permute-start(bf16[128,4096]{1,0:T(8,128)(2,1)S(1)} %pad_maximum_fusion.2), channel_id=1, source_target_pairs={{0,16},{16,0},{1,17},{17,1},{2,18},{18,2},{3,19},{19,3},{4,20},{20... | collective-permute-start | bytes 3145736 | tf_op jit(solution)/shard_map/ppermute | solution.py:23
  151.3 26.4 %collective-permute-start.40 = (bf16[512,512]{1,0:T(8,128)(2,1)S(1)}, bf16[512,512]{1,0:T(8,128)(2,1)S(1)}, u32[]{:S(2)}, u32[]{:S(2)}) collective-permute-start(bf16[512,512]{1,0:T(8,128)(2,1)S(1)} %get-tuple-element.317), channel_id=1, source_target_pairs={{4,8},{8,4},{5,9},{9,5},{6,10},{10,6},{7,11},{11,7},{20,24},{24,20... | collective-permute-start | bytes 1572872 | tf_op jit(solution)/shard_map/ppermute | solution.py:347
  160.9 16.8 %collective-permute-start.38 = (bf16[512,512]{1,0:T(8,128)(2,1)S(1)}, bf16[512,512]{1,0:T(8,128)(2,1)S(1)}, u32[]{:S(2)}, u32[]{:S(2)}) collective-permute-start(bf16[512,512]{1,0:T(8,128)(2,1)S(1)} %fusion.16), channel_id=1, source_target_pairs={{0,4},{4,0},{8,12},{12,8},{1,5},{5,1},{9,13},{13,9},{2,6},{6,2},{1... | collective-permute-start | bytes 1572872 | tf_op jit(solution)/shard_map/ppermute | solution.py:23
  (18 other events, 108.0 us)

commit v2 on v1

--- a/solution.py
+++ b/solution.py
@@ -46,8 +46,9 @@
     )
 
 
-def attend_kernel(visible, query, key_early, key_late, value_early, value_late, upstream, *refs):
-    attended, query_grad, kv_grad = refs[-3:]
+def attend_kernel(
+    visible, query, key_early, key_late, value_early, value_late, upstream, attended, query_grad, kv_grad
+):
     score_scale = HD ** (-0.5)
     query_rows, upstream_rows = query[...], upstream[...]
     key_rows = jnp.concatenate([key_early[...], key_late[...]], axis=0)
@@ -66,7 +67,7 @@
     query_grad[...] = dot(grad_scores, key_rows, 0, 0).astype(BF16)
 
 
-def attend_head(head, visible, query, key_early, key_late, value_early, value_late, upstream, kept):
+def attend_head(head, visible, query, key_early, key_late, value_early, value_late, upstream):
     src_rows, target_rows = visible.shape[0], query.shape[0]
     early, late = key_early.shape[0], key_late.shape[0]
 
@@ -87,18 +88,16 @@
             column(early),
             column(late),
             column(target_rows),
-        ]
-        + [pl.BlockSpec(memory_space=pl.ANY)] * len(kept),
-        out_specs=[column(target_rows), column(target_rows), whole(src_rows, 2 * HD)],
+        ],
+        out_specs=[whole(target_rows, HD), whole(target_rows, HD), whole(src_rows, 2 * HD)],
         out_shape=[
-            jax.ShapeDtypeStruct(query.shape, BF16),
-            jax.ShapeDtypeStruct(query.shape, BF16),
+            jax.ShapeDtypeStruct((target_rows, HD), BF16),
+            jax.ShapeDtypeStruct((target_rows, HD), BF16),
             jax.ShapeDtypeStruct((src_rows, 2 * HD), BF16),
         ],
-        input_output_aliases={7 + slot: slot for slot in range(len(kept))},
         compiler_params=pltpu.CompilerParams(vmem_limit_bytes=6 * MIB + 40 * src_rows * target_rows),
         cost_estimate=FILLS_WAITS,
-    )(visible, query, key_early, key_late, value_early, value_late, upstream, *kept)
+    )(visible, query, key_early, key_late, value_early, value_late, upstream)
 
 
 def row_kernel(head_count, *refs):
@@ -235,12 +234,9 @@
 
     held["key_early"] = key_early
 
-    outputs = []
-
     def attend(head):
-        early_keys = held["key_early"]
-        *outputs[:], held[("kv", head)] = attend_head(
-            head, visible, queries[0], early_keys, key_late, value_early, value_late, out_grad[0], list(outputs)
+        held[("attended", head)], held[("query", head)], held[("kv", head)] = attend_head(
+            head, visible, queries[0], held["key_early"], key_late, value_early, value_late, out_grad[0]
         )
 
     def hand_in(head):
@@ -376,7 +372,11 @@
     if not by_steps:
         held["row_low"] = row_product([held[("kv", head)] for head in heads], key_weight, value_weight, 0, 2)
         held["row_high"] = row_product([held[("kv", head)] for head in heads], key_weight, value_weight, 1, 2)
-    sync(*kinds("outward", "relay"), *(("inner", head) for head in heads[:-1]), *kinds("kv", "their"))
+    sync(("relay", last - 1), *kinds("attended", "query"))
+    for name in ("attended", "query"):
+        held[name] = jnp.concatenate([held[(name, head)] for head in heads], axis=1)
+    ends = ["attended", "query", *kinds("outward", "relay"), *(("inner", head) for head in heads[:-1])]
+    sync(*ends, *kinds("kv", "their"))
     relay(last)
     for head in heads[:-1]:
         finish(head)
@@ -386,11 +386,11 @@
     sync(("relay", last), "enc_grad")
     finish(last)
     return (
-        outputs[0][None],
+        held["attended"][None],
         held["enc_grad"][None],
         held[("total", 0)],
         held[("total", 1)],
-        outputs[1][None],
+        held["query"][None],
     )
 
 

time: 183 us -> 180 us (0.984)
  Pallas kernels: 23.7 us -> 20.8 us
  other arithmetic: 8.21 us -> 10.4 us
    pallas_call x4, Pallas kernels: 8.87 us -> 6.04 us  [attend_head(): pl.pallas_call(attend_kernel, grid=(1,), in_specs=[whole(src_rows, 1), co...]
    concatenate x0 -> x2, other arithmetic: none -> 2.22 us  [on_device(): held[name] = jnp.concatenate([held[name, head] for head in heads], axis=1)]
  transfers between devices with their start and end apart: 41 -> 41, of which waited for: 12 -> 12; matrix products, arithmetic and copies ran while one was open for 27% -> 28% of each run, Pallas kernels for 13% -> 11%
where the time goes in v2:
time: 180 us; the launch traced here: 177 us
  waiting for transfers between devices  50 us (28%)
  starting transfers between devices  49.8 us (28%)
  matrix products  36.8 us (20%)
  Pallas kernels  20.8 us (12%)
  other arithmetic  10.4 us (6%)
  local copies, waits for them, and re-layouts  6.81 us (4%)
  between operations  1.81 us (1%)
    ppermute x31, starting transfers between devices, swap(): return lax.ppermute(value, axis, pairs)  40 us
    ppermute x31, waiting for transfers between devices, swap(): return lax.ppermute(value, axis, pairs)  32.3 us
    dot_general x40, matrix products, dot(): lax.dot_general(left, right, (((left_dim,), (right_dim,)), ((), ())), pre...  23.7 us
    ppermute x2, waiting for transfers between devices, swap_both(): return lax.ppermute(rows, ('section', 'seq'), pairs)  17.8 us
    pallas_call x2, Pallas kernels, row_product(): pl.pallas_call(functools.partial(row_kernel, len(grads)), grid=(steps,),...  10.5 us
    dot_general x1, matrix products, on_device(): jnp.dot(early, key_weight, preferred_element_type=F32).astype(BF16)  7.28 us
    pallas_call x4, Pallas kernels, attend_head(): pl.pallas_call(attend_kernel, grid=(1,), in_specs=[whole(src_rows, 1), co...  6.04 us
    pallas_call x4, Pallas kernels, add_columns(): pl.pallas_call(functools.partial(add_kernel, count), grid=(1,), in_specs=...  4.26 us
  transfers between devices with their start and end apart: 41, of which 12 were waited for; matrix products, arithmetic and copies ran while one was open for 28% of the time, Pallas kernels for 11%

profile of v2, /device:TPU:0, one launch (start us, length us, event | category | flops | bytes accessed | tf_op | source)
XLA Modules:
  0.0 176.5 jit_solution(10707320864039664756)
XLA Ops:
  0.6 1.5 fusion
  2.2 1.6 fusion.2
  4.3 2.6 %collective-permute-start.1 = (bf16[128,4096]{1,0:T(8,128)(2,1)S(1)}, bf16[128,4096]{1,0:T(8,128)(2,1)S(1)}, u32[]{:S(2)}, u32[]{:S(2)}) collective-permute-start(bf16[128,4096]{1,0:T(8,128)(2,1)S(1)} %fusion.2), channel_id=1, source_target_pairs={{0,17},{1,16},{2,19},{3,18},{16,1},{17,0},{18,3},{19,2},{4,21},{5,... | collective-permute-start | bytes 3145736 | tf_op jit(solution)/shard_map/ppermute | solution.py:193
  10.6 1.6 collective-permute-start.3
  14.3 16.0 %collective-permute-done.1 = bf16[128,4096]{1,0:T(8,128)(2,1)S(1)} collective-permute-done((bf16[128,4096]{1,0:T(8,128)(2,1)S(1)}, bf16[128,4096]{1,0:T(8,128)(2,1)S(1)}, u32[]{:S(2)}, u32[]{:S(2)}) %collective-permute-start.1) | collective-permute-done | bytes 1048608 | tf_op jit(solution)/shard_map/ppermute | solution.py:193
  30.3 1.8 %collective-permute-done.2 = bf16[128,4096]{1,0:T(8,128)(2,1)S(1)} collective-permute-done((bf16[128,4096]{1,0:T(8,128)(2,1)S(1)}, bf16[128,4096]{1,0:T(8,128)(2,1)S(1)}, u32[]{:S(2)}, u32[]{:S(2)}) %collective-permute-start.2) | collective-permute-done | bytes 1048608 | tf_op jit(solution)/shard_map/ppermute | solution.py:193
  32.7 1.6 collective-permute-start.5
  34.7 7.3 %convolution_convert_fusion.1.key_early = bf16[384,1024]{1,0:T(8,128)(2,1)S(1)} fusion(bf16[384,4096]{1,0:T(8,128)(2,1)S(1)} %constant_dynamic-update-slice_fusion, bf16[4096,1024]{1,0:T(8,128)(2,1)} %refs_4_.3), kind=kOutput, calls=%fused_computation.27 | convolution fusion | flops 3221618688 | bytes 12320768 | tf_op jit(solution)/shard_map/dot_general | solution.py:221
  42.1 3.4 %convolution_convert_fusion.value_early = bf16[384,1024]{1,0:T(8,128)(2,1)S(1)} fusion(bf16[384,4096]{1,0:T(8,128)(2,1)S(1)} %constant_dynamic-update-slice_fusion, bf16[4096,1024]{1,0:T(8,128)(2,1)S(1)} %bitcast.67), kind=kOutput, calls=%fused_computation.26 | convolution fusion | flops 3221618688 | bytes 12320768 | tf_op jit(solution)/shard_map/dot_general | solution.py:220
  52.0 1.5 shard_map.110
  53.5 1.9 %collective-permute-start.10 = (bf16[512,512]{1,0:T(8,128)(2,1)S(1)}, bf16[512,512]{1,0:T(8,128)(2,1)S(1)}, u32[]{:S(2)}, u32[]{:S(2)}) collective-permute-start(bf16[512,512]{1,0:T(8,128)(2,1)S(1)} %get-tuple-element.322.refs_0_), channel_id=1, source_target_pairs={{0,4},{4,0},{8,12},{12,8},{1,5},{5,1},{9,13},{13,9},{2,6},{6,2},{1... | collective-permute-start | bytes 1572872 | tf_op jit(solution)/shard_map/ppermute | solution.py:23
  56.4 5.0 %collective-permute-done.7 = bf16[256,1024]{1,0:T(8,128)(2,1)S(1)} collective-permute-done((bf16[256,1024]{1,0:T(8,128)(2,1)}, bf16[256,1024]{1,0:T(8,128)(2,1)S(1)}, u32[]{:S(2)}, u32[]{:S(2)}) %collective-permute-start.7) | collective-permute-done | bytes 524320 | tf_op jit(solution)/shard_map/ppermute | solution.py:23
  62.4 1.6 collective-permute-start.13
  66.5 1.5 shard_map.112
  68.0 1.7 shard_map.113
  69.8 1.6 collective-permute-start.19
  77.1 4.4 %collective-permute-start.21 = (bf16[512,512]{1,0:T(8,128)(2,1)S(1)}, bf16[512,512]{1,0:T(8,128)(2,1)S(1)}, u32[]{:S(2)}, u32[]{:S(2)}) collective-permute-start(bf16[512,512]{1,0:T(8,128)(2,1)S(1)} %get-tuple-element.314.refs_2_), channel_id=1, source_target_pairs={{0,4},{4,0},{8,12},{12,8},{1,5},{5,1},{9,13},{13,9},{2,6},{6,2},{1... | collective-permute-start | bytes 1572872 | tf_op jit(solution)/shard_map/ppermute | solution.py:23
  82.2 5.3 %shard_map.114 = bf16[512,2048]{1,0:T(8,128)(2,1)S(1)} custom-call(bf16[512,512]{1,0:T(8,128)(2,1)S(1)} %get-tuple-element.322.refs_0_, bf16[512,512]{1,0:T(8,128)(2,1)S(1)} %get-tuple-element.318.refs_1_, bf16[512,512]{1,0:T(8,128)(2,1)S(1)} %get-tuple-element.314.refs_2_, bf16[512,512]{1,0:T(8,128)(2,1)S(1)} %get-tuple-element.304.refs_3_, ...), custom_call_target="tpu_custom_call" | custom-call | flops 4294967296 | bytes 11534336 | tf_op jit(solution)/shard_map/pallas_call | solution.py:118
  88.3 5.2 %shard_map.115 = bf16[512,2048]{1,0:T(8,128)(2,1)S(1)} custom-call(bf16[512,512]{1,0:T(8,128)(2,1)S(1)} %get-tuple-element.322.refs_0_, bf16[512,512]{1,0:T(8,128)(2,1)S(1)} %get-tuple-element.318.refs_1_, bf16[512,512]{1,0:T(8,128)(2,1)S(1)} %get-tuple-element.314.refs_2_, bf16[512,512]{1,0:T(8,128)(2,1)S(1)} %get-tuple-element.304.refs_3_, ...), custom_call_target="tpu_custom_call" | custom-call | flops 4294967296 | bytes 11534336 | tf_op jit(solution)/shard_map/pallas_call | solution.py:118
  93.6 1.5 collective-permute-start.26
  102.8 4.6 %collective-permute-start.27 = (bf16[512,512]{1,0:T(8,128)(2,1)S(1)}, bf16[512,512]{1,0:T(8,128)(2,1)S(1)}, u32[]{:S(2)}, u32[]{:S(2)}) collective-permute-start(bf16[512,512]{1,0:T(8,128)(2,1)S(1)} %get-tuple-element.304.refs_3_), channel_id=1, source_target_pairs={{0,4},{4,0},{8,12},{12,8},{1,5},{5,1},{9,13},{13,9},{2,6},{6,2},{1... | collective-permute-start | bytes 1572872 | tf_op jit(solution)/shard_map/ppermute | solution.py:23
  107.3 5.2 %collective-permute-done.24 = bf16[256,2048]{1,0:T(8,128)(2,1)S(1)} collective-permute-done((bf16[256,2048]{1,0:T(8,128)(2,1)S(1)}, bf16[256,2048]{1,0:T(8,128)(2,1)S(1)}, u32[]{:S(2)}, u32[]{:S(2)}) %collective-permute-start.24) | collective-permute-done | bytes 1048608 | tf_op jit(solution)/shard_map/ppermute | solution.py:23
  113.4 4.6 %collective-permute-start.30 = (bf16[512,512]{1,0:T(8,128)(2,1)S(1)}, bf16[512,512]{1,0:T(8,128)(2,1)S(1)}, u32[]{:S(2)}, u32[]{:S(2)}) collective-permute-start(bf16[512,512]{1,0:T(8,128)(2,1)S(1)} %fusion.13), channel_id=1, source_target_pairs={{0,4},{4,0},{8,12},{12,8},{1,5},{5,1},{9,13},{13,9},{2,6},{6,2},{1... | collective-permute-start | bytes 1572872 | tf_op jit(solution)/shard_map/ppermute | solution.py:23
  123.8 2.5 %collective-permute-start.32 = (bf16[512,512]{1,0:T(8,128)(2,1)S(1)}, bf16[512,512]{1,0:T(8,128)(2,1)S(1)}, u32[]{:S(2)}, u32[]{:S(2)}) collective-permute-start(bf16[512,512]{1,0:T(8,128)(2,1)S(1)} %fusion.14), channel_id=1, source_target_pairs={{0,4},{4,0},{8,12},{12,8},{1,5},{5,1},{9,13},{13,9},{2,6},{6,2},{1... | collective-permute-start | bytes 1572872 | tf_op jit(solution)/shard_map/ppermute | solution.py:23
  127.5 3.8 %collective-permute-done.30.second = bf16[512,512]{1,0:T(8,128)(2,1)S(1)} collective-permute-done((bf16[512,512]{1,0:T(8,128)(2,1)S(1)}, bf16[512,512]{1,0:T(8,128)(2,1)S(1)}, u32[]{:S(2)}, u32[]{:S(2)}) %collective-permute-start.30) | collective-permute-done | bytes 524320 | tf_op jit(solution)/shard_map/ppermute | solution.py:23
  131.3 1.5 collective-permute-start.34
  136.5 5.1 %collective-permute-done.32.second = bf16[512,512]{1,0:T(8,128)(2,1)S(1)} collective-permute-done((bf16[512,512]{1,0:T(8,128)(2,1)S(1)}, bf16[512,512]{1,0:T(8,128)(2,1)S(1)}, u32[]{:S(2)}, u32[]{:S(2)}) %collective-permute-start.32) | collective-permute-done | bytes 524320 | tf_op jit(solution)/shard_map/ppermute | solution.py:23
  141.6 1.8 collective-permute-done.34
  144.3 1.5 collective-permute-start.35
  148.2 7.4 %collective-permute-done.35.second = bf16[512,512]{1,0:T(8,128)(2,1)S(1)} collective-permute-done((bf16[512,512]{1,0:T(8,128)(2,1)S(1)}, bf16[512,512]{1,0:T(8,128)(2,1)S(1)}, u32[]{:S(2)}, u32[]{:S(2)}) %collective-permute-start.35) | collective-permute-done | bytes 524320 | tf_op jit(solution)/shard_map/ppermute | solution.py:23
  158.8 5.4 %collective-permute-start.38 = (bf16[512,512]{1,0:T(8,128)(2,1)S(1)}, bf16[512,512]{1,0:T(8,128)(2,1)S(1)}, u32[]{:S(2)}, u32[]{:S(2)}) collective-permute-start(bf16[512,512]{1,0:T(8,128)(2,1)S(1)} %fusion.16), channel_id=1, source_target_pairs={{0,4},{4,0},{8,12},{12,8},{1,5},{5,1},{9,13},{13,9},{2,6},{6,2},{1... | collective-permute-start | bytes 1572872 | tf_op jit(solution)/shard_map/ppermute | solution.py:23
  172.4 1.7 fusion.7
  (170 shorter events, 61.4 us)
Async XLA Ops:
  4.3 26.1 %collective-permute-start.1 = (bf16[128,4096]{1,0:T(8,128)(2,1)S(1)}, bf16[128,4096]{1,0:T(8,128)(2,1)S(1)}, u32[]{:S(2)}, u32[]{:S(2)}) collective-permute-start(bf16[128,4096]{1,0:T(8,128)(2,1)S(1)} %fusion.2), channel_id=1, source_target_pairs={{0,17},{1,16},{2,19},{3,18},{16,1},{17,0},{18,3},{19,2},{4,21},{5,... | collective-permute-start | bytes 3145736 | tf_op jit(solution)/shard_map/ppermute | solution.py:193
  6.9 25.2 %collective-permute-start.2 = (bf16[128,4096]{1,0:T(8,128)(2,1)S(1)}, bf16[128,4096]{1,0:T(8,128)(2,1)S(1)}, u32[]{:S(2)}, u32[]{:S(2)}) collective-permute-start(bf16[128,4096]{1,0:T(8,128)(2,1)S(1)} %fusion.2), channel_id=1, source_target_pairs={{0,18},{1,19},{2,16},{3,17},{16,2},{17,3},{18,0},{19,1},{4,22},{5,... | collective-permute-start | bytes 3145736 | tf_op jit(solution)/shard_map/ppermute | solution.py:193
  10.6 21.5 %collective-permute-start.3 = (bf16[256,1024]{1,0:T(8,128)(2,1)}, bf16[256,1024]{1,0:T(8,128)(2,1)}, u32[]{:S(2)}, u32[]{:S(2)}) collective-permute-start(bf16[256,1024]{1,0:T(8,128)(2,1)} %maximum_maximum_fusion), channel_id=1, source_target_pairs={{0,4},{4,0},{8,12},{12,8},{1,5},{5,1},{9,13},{13,9},{2,6},{6,2},{1... | collective-permute-start | bytes 1572872 | tf_op jit(solution)/shard_map/ppermute | solution.py:23
  32.5 15.6 %collective-permute-start.4 = (bf16[256,2048]{1,0:T(8,128)(2,1)S(1)}, bf16[256,2048]{1,0:T(8,128)(2,1)S(1)}, u32[]{:S(2)}, u32[]{:S(2)}) collective-permute-start(bf16[256,2048]{1,0:T(8,128)(2,1)S(1)} %fusion.17), channel_id=1, source_target_pairs={{0,16},{16,0},{1,17},{17,1},{2,18},{18,2},{3,19},{19,3},{4,20},{20... | collective-permute-start | bytes 3145736 | tf_op jit(solution)/shard_map/ppermute | solution.py:23
  32.7 14.2 %collective-permute-start.5 = (bf16[64,4096]{1,0:T(8,128)(2,1)S(1)}, bf16[64,4096]{1,0:T(8,128)(2,1)S(1)}, u32[]{:S(2)}, u32[]{:S(2)}) collective-permute-start(bf16[64,4096]{1,0:T(8,128)(2,1)S(1)} %slice.169), channel_id=1, source_target_pairs={{0,2},{1,3},{2,0},{3,1},{4,6},{5,7},{6,4},{7,5},{8,10},{9,11},{10,... | collective-permute-start | bytes 1572872 | tf_op jit(solution)/shard_map/ppermute | solution.py:23
  34.2 13.9 %collective-permute-start.6 = (bf16[64,4096]{1,0:T(8,128)(2,1)S(1)}, bf16[64,4096]{1,0:T(8,128)(2,1)S(1)}, u32[]{:S(2)}, u32[]{:S(2)}) collective-permute-start(bf16[64,4096]{1,0:T(8,128)(2,1)S(1)} %slice.170), channel_id=1, source_target_pairs={{0,1},{1,0},{2,3},{3,2},{4,5},{5,4},{6,7},{7,6},{8,9},{9,8},{10,11... | collective-permute-start | bytes 1572872 | tf_op jit(solution)/shard_map/ppermute | solution.py:23
  48.1 13.3 %collective-permute-start.7 = (bf16[256,1024]{1,0:T(8,128)(2,1)}, bf16[256,1024]{1,0:T(8,128)(2,1)S(1)}, u32[]{:S(2)}, u32[]{:S(2)}) collective-permute-start(bf16[256,1024]{1,0:T(8,128)(2,1)} %collective-permute-done.3), channel_id=1, source_target_pairs={{0,1},{1,0},{2,3},{3,2},{4,5},{5,4},{6,7},{7,6},{8,9},{9,8},{10,11... | collective-permute-start | bytes 1572872 | tf_op jit(solution)/shard_map/ppermute | solution.py:23
  48.7 13.0 %collective-permute-start.8 = (bf16[256,1024]{1,0:T(8,128)(2,1)}, bf16[256,1024]{1,0:T(8,128)(2,1)S(1)}, u32[]{:S(2)}, u32[]{:S(2)}) collective-permute-start(bf16[256,1024]{1,0:T(8,128)(2,1)} %collective-permute-done.3), channel_id=1, source_target_pairs={{0,2},{1,3},{2,0},{3,1},{4,6},{5,7},{6,4},{7,5},{8,10},{9,11},{10,... | collective-permute-start | bytes 1572872 | tf_op jit(solution)/shard_map/ppermute | solution.py:23
  53.5 16.4 %collective-permute-start.10 = (bf16[512,512]{1,0:T(8,128)(2,1)S(1)}, bf16[512,512]{1,0:T(8,128)(2,1)S(1)}, u32[]{:S(2)}, u32[]{:S(2)}) collective-permute-start(bf16[512,512]{1,0:T(8,128)(2,1)S(1)} %get-tuple-element.322.refs_0_), channel_id=1, source_target_pairs={{0,4},{4,0},{8,12},{12,8},{1,5},{5,1},{9,13},{13,9},{2,6},{6,2},{1... | collective-permute-start | bytes 1572872 | tf_op jit(solution)/shard_map/ppermute | solution.py:23
  55.3 16.2 %collective-permute-start.11 = (bf16[512,512]{1,0:T(8,128)(2,1)S(1)}, bf16[512,512]{1,0:T(8,128)(2,1)S(1)}, u32[]{:S(2)}, u32[]{:S(2)}) collective-permute-start(bf16[512,512]{1,0:T(8,128)(2,1)S(1)} %get-tuple-element.322.refs_0_), channel_id=1, source_target_pairs={{0,16},{16,0},{1,17},{17,1},{2,18},{18,2},{3,19},{19,3},{4,20},{20... | collective-permute-start | bytes 1572872 | tf_op jit(solution)/shard_map/ppermute | solution.py:23
  69.8 23.8 %collective-permute-start.19 = (bf16[512,512]{1,0:T(8,128)(2,1)S(1)}, bf16[512,512]{1,0:T(8,128)(2,1)S(1)}, u32[]{:S(2)}, u32[]{:S(2)}) collective-permute-start(bf16[512,512]{1,0:T(8,128)(2,1)S(1)} %get-tuple-element.318.refs_1_), channel_id=1, source_target_pairs={{0,4},{4,0},{8,12},{12,8},{1,5},{5,1},{9,13},{13,9},{2,6},{6,2},{1... | collective-permute-start | bytes 1572872 | tf_op jit(solution)/shard_map/ppermute | solution.py:23
  76.4 18.8 %collective-permute-start.18 = (bf16[512,512]{1,0:T(8,128)(2,1)S(1)}, bf16[512,512]{1,0:T(8,128)(2,1)S(1)}, u32[]{:S(2)}, u32[]{:S(2)}) collective-permute-start(bf16[512,512]{1,0:T(8,128)(2,1)S(1)} %get-tuple-element.348), channel_id=1, source_target_pairs={{4,8},{8,4},{5,9},{9,5},{6,10},{10,6},{7,11},{11,7},{20,24},{24,20... | collective-permute-start | bytes 1572872 | tf_op jit(solution)/shard_map/ppermute | solution.py:342
  77.1 22.2 %collective-permute-start.21 = (bf16[512,512]{1,0:T(8,128)(2,1)S(1)}, bf16[512,512]{1,0:T(8,128)(2,1)S(1)}, u32[]{:S(2)}, u32[]{:S(2)}) collective-permute-start(bf16[512,512]{1,0:T(8,128)(2,1)S(1)} %get-tuple-element.314.refs_2_), channel_id=1, source_target_pairs={{0,4},{4,0},{8,12},{12,8},{1,5},{5,1},{9,13},{13,9},{2,6},{6,2},{1... | collective-permute-start | bytes 1572872 | tf_op jit(solution)/shard_map/ppermute | solution.py:23
  81.5 21.3 %collective-permute-start.23 = (bf16[512,512]{1,0:T(8,128)(2,1)S(1)}, bf16[512,512]{1,0:T(8,128)(2,1)S(1)}, u32[]{:S(2)}, u32[]{:S(2)}) collective-permute-start(bf16[512,512]{1,0:T(8,128)(2,1)S(1)} %get-tuple-element.347), channel_id=1, source_target_pairs={{4,8},{8,4},{5,9},{9,5},{6,10},{10,6},{7,11},{11,7},{20,24},{24,20... | collective-permute-start | bytes 1572872 | tf_op jit(solution)/shard_map/ppermute | solution.py:343
  87.6 24.9 %collective-permute-start.24 = (bf16[256,2048]{1,0:T(8,128)(2,1)S(1)}, bf16[256,2048]{1,0:T(8,128)(2,1)S(1)}, u32[]{:S(2)}, u32[]{:S(2)}) collective-permute-start(bf16[256,2048]{1,0:T(8,128)(2,1)S(1)} %pad_maximum_fusion.1), channel_id=1, source_target_pairs={{0,1},{1,0},{2,3},{3,2},{4,5},{5,4},{6,7},{7,6},{8,9},{9,8},{10,11... | collective-permute-start | bytes 3145736 | tf_op jit(solution)/shard_map/ppermute | solution.py:23
  93.6 27.2 %collective-permute-start.26 = (bf16[256,2048]{1,0:T(8,128)(2,1)S(1)}, bf16[256,2048]{1,0:T(8,128)(2,1)S(1)}, u32[]{:S(2)}, u32[]{:S(2)}) collective-permute-start(bf16[256,2048]{1,0:T(8,128)(2,1)S(1)} %concatenate.61), channel_id=1, source_target_pairs={{0,2},{1,3},{2,0},{3,1},{4,6},{5,7},{6,4},{7,5},{8,10},{9,11},{10,... | collective-permute-start | bytes 3145736 | tf_op jit(solution)/shard_map/ppermute | solution.py:23
  99.3 14.2 %collective-permute-start.22 = (bf16[512,512]{1,0:T(8,128)(2,1)S(1)}, bf16[512,512]{1,0:T(8,128)(2,1)S(1)}, u32[]{:S(2)}, u32[]{:S(2)}) collective-permute-start(bf16[512,512]{1,0:T(8,128)(2,1)S(1)} %collective-permute-done.21), channel_id=1, source_target_pairs={{0,16},{16,0},{1,17},{17,1},{2,18},{18,2},{3,19},{19,3},{4,20},{20... | collective-permute-start | bytes 1572872 | tf_op jit(solution)/shard_map/ppermute | solution.py:23
  99.9 20.9 %collective-permute-start.25 = (bf16[512,512]{1,0:T(8,128)(2,1)S(1)}, bf16[512,512]{1,0:T(8,128)(2,1)S(1)}, u32[]{:S(2)}, u32[]{:S(2)}) collective-permute-start(bf16[512,512]{1,0:T(8,128)(2,1)S(1)} %get-tuple-element.346), channel_id=1, source_target_pairs={{4,8},{8,4},{5,9},{9,5},{6,10},{10,6},{7,11},{11,7},{20,24},{24,20... | collective-permute-start | bytes 1572872 | tf_op jit(solution)/shard_map/ppermute | solution.py:342
  102.8 18.1 %collective-permute-start.27 = (bf16[512,512]{1,0:T(8,128)(2,1)S(1)}, bf16[512,512]{1,0:T(8,128)(2,1)S(1)}, u32[]{:S(2)}, u32[]{:S(2)}) collective-permute-start(bf16[512,512]{1,0:T(8,128)(2,1)S(1)} %get-tuple-element.304.refs_3_), channel_id=1, source_target_pairs={{0,4},{4,0},{8,12},{12,8},{1,5},{5,1},{9,13},{13,9},{2,6},{6,2},{1... | collective-permute-start | bytes 1572872 | tf_op jit(solution)/shard_map/ppermute | solution.py:23
  112.5 14.1 %collective-permute-start.29 = (bf16[512,512]{1,0:T(8,128)(2,1)S(1)}, bf16[512,512]{1,0:T(8,128)(2,1)S(1)}, u32[]{:S(2)}, u32[]{:S(2)}) collective-permute-start(bf16[512,512]{1,0:T(8,128)(2,1)S(1)} %get-tuple-element.345), channel_id=1, source_target_pairs={{4,8},{8,4},{5,9},{9,5},{6,10},{10,6},{7,11},{11,7},{20,24},{24,20... | collective-permute-start | bytes 1572872 | tf_op jit(solution)/shard_map/ppermute | solution.py:343
  113.4 17.9 %collective-permute-start.30 = (bf16[512,512]{1,0:T(8,128)(2,1)S(1)}, bf16[512,512]{1,0:T(8,128)(2,1)S(1)}, u32[]{:S(2)}, u32[]{:S(2)}) collective-permute-start(bf16[512,512]{1,0:T(8,128)(2,1)S(1)} %fusion.13), channel_id=1, source_target_pairs={{0,4},{4,0},{8,12},{12,8},{1,5},{5,1},{9,13},{13,9},{2,6},{6,2},{1... | collective-permute-start | bytes 1572872 | tf_op jit(solution)/shard_map/ppermute | solution.py:23
  120.8 12.0 %collective-permute-start.28 = (bf16[512,512]{1,0:T(8,128)(2,1)S(1)}, bf16[512,512]{1,0:T(8,128)(2,1)S(1)}, u32[]{:S(2)}, u32[]{:S(2)}) collective-permute-start(bf16[512,512]{1,0:T(8,128)(2,1)S(1)} %collective-permute-done.27), channel_id=1, source_target_pairs={{0,16},{16,0},{1,17},{17,1},{2,18},{18,2},{3,19},{19,3},{4,20},{20... | collective-permute-start | bytes 1572872 | tf_op jit(solution)/shard_map/ppermute | solution.py:23
  122.2 14.3 %collective-permute-start.31 = (bf16[512,512]{1,0:T(8,128)(2,1)S(1)}, bf16[512,512]{1,0:T(8,128)(2,1)S(1)}, u32[]{:S(2)}, u32[]{:S(2)}) collective-permute-start(bf16[512,512]{1,0:T(8,128)(2,1)S(1)} %get-tuple-element.344), channel_id=1, source_target_pairs={{4,8},{8,4},{5,9},{9,5},{6,10},{10,6},{7,11},{11,7},{20,24},{24,20... | collective-permute-start | bytes 1572872 | tf_op jit(solution)/shard_map/ppermute | solution.py:342
  123.8 17.8 %collective-permute-start.32 = (bf16[512,512]{1,0:T(8,128)(2,1)S(1)}, bf16[512,512]{1,0:T(8,128)(2,1)S(1)}, u32[]{:S(2)}, u32[]{:S(2)}) collective-permute-start(bf16[512,512]{1,0:T(8,128)(2,1)S(1)} %fusion.14), channel_id=1, source_target_pairs={{0,4},{4,0},{8,12},{12,8},{1,5},{5,1},{9,13},{13,9},{2,6},{6,2},{1... | collective-permute-start | bytes 1572872 | tf_op jit(solution)/shard_map/ppermute | solution.py:23
  126.7 14.9 %collective-permute-start.33 = (bf16[128,2048]{1,0:T(8,128)(2,1)S(1)}, bf16[128,2048]{1,0:T(8,128)(2,1)S(1)}, u32[]{:S(2)}, u32[]{:S(2)}) collective-permute-start(bf16[128,2048]{1,0:T(8,128)(2,1)S(1)} %add_convert_fusion.7), channel_id=1, source_target_pairs={{0,2},{1,3},{2,0},{3,1},{4,6},{5,7},{6,4},{7,5},{8,10},{9,11},{10,... | collective-permute-start | bytes 1572872 | tf_op jit(solution)/shard_map/ppermute | solution.py:23
  131.3 12.0 %collective-permute-start.34 = (bf16[128,2048]{1,0:T(8,128)(2,1)S(1)}, bf16[128,2048]{1,0:T(8,128)(2,1)S(1)}, u32[]{:S(2)}, u32[]{:S(2)}) collective-permute-start(bf16[128,2048]{1,0:T(8,128)(2,1)S(1)} %add_convert_fusion.6), channel_id=1, source_target_pairs={{0,1},{1,0},{2,3},{3,2},{4,5},{5,4},{6,7},{7,6},{8,9},{9,8},{10,11... | collective-permute-start | bytes 1572872 | tf_op jit(solution)/shard_map/ppermute | solution.py:23
  132.8 25.0 %collective-permute-start.37 = (bf16[512,512]{1,0:T(8,128)(2,1)S(1)}, bf16[512,512]{1,0:T(8,128)(2,1)S(1)}, u32[]{:S(2)}, u32[]{:S(2)}) collective-permute-start(bf16[512,512]{1,0:T(8,128)(2,1)S(1)} %get-tuple-element.343), channel_id=1, source_target_pairs={{4,8},{8,4},{5,9},{9,5},{6,10},{10,6},{7,11},{11,7},{20,24},{24,20... | collective-permute-start | bytes 1572872 | tf_op jit(solution)/shard_map/ppermute | solution.py:343
  144.3 11.3 %collective-permute-start.35 = (bf16[512,512]{1,0:T(8,128)(2,1)S(1)}, bf16[512,512]{1,0:T(8,128)(2,1)S(1)}, u32[]{:S(2)}, u32[]{:S(2)}) collective-permute-start(bf16[512,512]{1,0:T(8,128)(2,1)S(1)} %fusion.15), channel_id=1, source_target_pairs={{0,4},{4,0},{8,12},{12,8},{1,5},{5,1},{9,13},{13,9},{2,6},{6,2},{1... | collective-permute-start | bytes 1572872 | tf_op jit(solution)/shard_map/ppermute | solution.py:23
  145.9 12.0 %collective-permute-start.36 = (bf16[512,512]{1,0:T(8,128)(2,1)S(1)}, bf16[512,512]{1,0:T(8,128)(2,1)S(1)}, u32[]{:S(2)}, u32[]{:S(2)}) collective-permute-start(bf16[512,512]{1,0:T(8,128)(2,1)S(1)} %get-tuple-element.342), channel_id=1, source_target_pairs={{4,8},{8,4},{5,9},{9,5},{6,10},{10,6},{7,11},{11,7},{20,24},{24,20... | collective-permute-start | bytes 1572872 | tf_op jit(solution)/shard_map/ppermute | solution.py:342
  147.1 24.0 %collective-permute-start.39 = (bf16[128,4096]{1,0:T(8,128)(2,1)S(1)}, bf16[128,4096]{1,0:T(8,128)(2,1)S(1)}, u32[]{:S(2)}, u32[]{:S(2)}) collective-permute-start(bf16[128,4096]{1,0:T(8,128)(2,1)S(1)} %pad_maximum_fusion.4), channel_id=1, source_target_pairs={{0,16},{16,0},{1,17},{17,1},{2,18},{18,2},{3,19},{19,3},{4,20},{20... | collective-permute-start | bytes 3145736 | tf_op jit(solution)/shard_map/ppermute | solution.py:23
  147.2 28.0 %collective-permute-start.40 = (bf16[512,512]{1,0:T(8,128)(2,1)S(1)}, bf16[512,512]{1,0:T(8,128)(2,1)S(1)}, u32[]{:S(2)}, u32[]{:S(2)}) collective-permute-start(bf16[512,512]{1,0:T(8,128)(2,1)S(1)} %get-tuple-element.341), channel_id=1, source_target_pairs={{4,8},{8,4},{5,9},{9,5},{6,10},{10,6},{7,11},{11,7},{20,24},{24,20... | collective-permute-start | bytes 1572872 | tf_op jit(solution)/shard_map/ppermute | solution.py:343
  158.8 16.4 %collective-permute-start.38 = (bf16[512,512]{1,0:T(8,128)(2,1)S(1)}, bf16[512,512]{1,0:T(8,128)(2,1)S(1)}, u32[]{:S(2)}, u32[]{:S(2)}) collective-permute-start(bf16[512,512]{1,0:T(8,128)(2,1)S(1)} %fusion.16), channel_id=1, source_target_pairs={{0,4},{4,0},{8,12},{12,8},{1,5},{5,1},{9,13},{13,9},{2,6},{6,2},{1... | collective-permute-start | bytes 1572872 | tf_op jit(solution)/shard_map/ppermute | solution.py:23
  (18 other events, 103.9 us)
